TPU v7x, 256 devices: a whole 4x4x8 slice. The times are simulated.
256 devices in a mesh: band: 8 (over x, core), tile: 32 (over z, y).
Axes of the slice: x: 4, y: 4, z: 8, core: 2. Of those that a mesh axis runs over, the one named last changes fastest.
Arguments:
- mean_state: float32 [256, 4096], P('band', 'tile'), may hold values from -6 to 6
- modes: float32 [256, 256, 4096], P(None, 'band', 'tile'), may hold values from -6 to 6
- east_vel: float32 [256, 4096], P('band', 'tile'), may hold values from -0.4 to 0.4
- north_vel: float32 [256, 4096], P('band', 'tile'), may hold values from -0.4 to 0.4
- sea_mask: int32 [256, 4096], P('band', 'tile'), may hold values 0 or 1
- obs_index: int32 [8, 32, 64], P('band', 'tile'), may hold values from 0 to 4095
- obs_value: float32 [8, 32, 64], P('band', 'tile'), may hold values from -6 to 6
- obs_weight: float32 [8, 32, 64], P('band', 'tile'), may hold values from 0.02 to 0.2
Outputs:
- mean_analysis: float32 [256, 4096], P('band', 'tile')
- basis: float32 [256, 256, 4096], P(None, 'band', 'tile')
- root_factor: float32 [256, 256], replicated
Inputs may be any that keep to these rules, and one draw needn't show every extreme that they name: `obs_index`: row-major index over the block's 32 x 128 points.
All inputs are finite; a program needn't handle non-finite values. No bound on the sum of `sea_mask` on one device may be relied on, other than what follows from the above.
Results may differ from a plain program's by a relative error of at most 0.000076.
Values sent between devices are 32-bit elements; how exact they have to be, the bound alone decides.
No kernel may reach another device: no remote copies, remote signals or barrier semaphores. Data moves between devices by JAX's collectives and lax.ppermute only.
A program may use at most 192 MiB of HBM per device.

v0:
```python
import jax
import jax.numpy as jnp
from jax import lax
from jax.sharding import PartitionSpec as P

HIGH = lax.Precision.HIGHEST


def with_halo(block, sides, width):
    for axis, dim in sides:
        count = lax.axis_size(axis)
        forward = [(i, i + 1) for i in range(count - 1)]
        backward = [(target, source) for source, target in forward]
        low = lax.ppermute(
            lax.slice_in_dim(block, block.shape[dim] - width, None, axis=dim), axis, forward
        )
        high = lax.ppermute(lax.slice_in_dim(block, 0, width, axis=dim), axis, backward)
        block = jnp.concatenate([low, block, high], axis=dim)
    return block


def inner_rows(first, second):
    return lax.dot_general(
        first, second, (((1,), (1,)), ((), ())), precision=HIGH, preferred_element_type=jnp.float32
    )


def factor_of(gram):
    return jnp.linalg.cholesky(lax.psum(gram, ("band", "tile")))


def chol_apply(factor, vector):
    half = lax.linalg.triangular_solve(factor, vector[:, None], left_side=True, lower=True)
    return lax.linalg.triangular_solve(factor, half, left_side=True, lower=True, transpose_a=True)[
        :, 0
    ]


def body(mean_state, modes, east_vel, north_vel, sea_mask, obs_index, obs_value, obs_weight):
    count = modes.shape[0]
    lat_rows = modes.shape[1]
    lon_cols = modes.shape[2]
    points = lat_rows * lon_cols
    fields = jnp.concatenate([mean_state[None], modes], axis=0)
    padded = with_halo(fields, (("band", 1), ("tile", 2)), 1)
    centre = padded[:, 1:-1, 1:-1]
    northern = padded[:, 2:, 1:-1]
    southern = padded[:, :-2, 1:-1]
    eastern = padded[:, 1:-1, 2:]
    western = padded[:, 1:-1, :-2]
    tendency = -0.5 * east_vel * (eastern - western) - 0.5 * north_vel * (northern - southern)
    tendency = tendency + 0.2 * (eastern + western + northern + southern - 4.0 * centre)
    advanced = sea_mask.astype(jnp.float32) * (centre + tendency)
    mean_fore = advanced[0].reshape(points)
    lmodes = advanced[1:].reshape(count, points)
    gram = inner_rows(lmodes, lmodes)
    indices = obs_index.reshape(-1)
    weights = obs_weight.reshape(-1)
    diff = obs_value.reshape(-1) - jnp.take(mean_fore, indices)
    identity = jnp.eye(count, dtype=jnp.float32)
    lower = factor_of(gram)
    qrows = lax.linalg.triangular_solve(lower, lmodes, left_side=True, lower=True)
    hq = jnp.take(qrows, indices, axis=1)
    local_c = inner_rows(hq * weights, hq)
    local_b = jnp.dot(hq, weights * diff, precision=HIGH, preferred_element_type=jnp.float32)
    c_total, b_total = lax.psum((local_c, local_b), ("band", "tile"))
    inner = jnp.dot(jnp.dot(lower, c_total, precision=HIGH), lower.T, precision=HIGH)
    amat = identity + inner / (count - 1.0)
    factor = jnp.linalg.cholesky(amat)
    solved = chol_apply(factor, jnp.dot(lower, b_total, precision=HIGH))
    coef = jnp.dot(lower.T, solved, precision=HIGH) / (count - 1.0)
    increment = jnp.dot(coef, qrows, precision=HIGH)
    total_points = points * lax.axis_size("band") * lax.axis_size("tile")
    scale = jnp.sqrt(jnp.float32(total_points))
    mean_analysis = (mean_fore + increment).reshape(lat_rows, lon_cols)
    basis = (qrows * scale).reshape(count, lat_rows, lon_cols)
    root_factor = lax.linalg.triangular_solve(factor, lower, left_side=True, lower=True).T / scale
    return (mean_analysis, basis, root_factor)


def solution(mesh):
    return jax.shard_map(
        body,
        mesh=mesh,
        in_specs=(
            P("band", "tile"),
            P(None, "band", "tile"),
            P("band", "tile"),
            P("band", "tile"),
            P("band", "tile"),
            P("band", "tile", None),
            P("band", "tile", None),
            P("band", "tile", None),
        ),
        out_specs=(P("band", "tile"), P(None, "band", "tile"), P()),
        check_vma=False,
    )
```

profile of v0, /device:TPU:1, one launch (start us, length us, event | category | flops | bytes accessed | tf_op | source)
XLA Modules:
  0.0 734.6 jit_solution(7527900217856621616)
XLA Ops:
  7.2 4.6 copy.27
  11.9 4.6 collective-permute-start
  18.6 4.3 collective-permute-done.1
  23.3 5.0 fusion.63
  36.8 4.2 collective-permute-start.3
  46.9 16.2 %add_multiply_fusion = f32[257,32,128]{2,0,1:T(8,128)S(1)} fusion(f32[1,32,128]{2,0,1:T(1,128)S(1)} %bitcast.172, f32[257,1,128]{2,0,1:T(8,128)S(1)} %collective-permute-done.1, f32[256,32,128]{2,0,1:T(8,128)} %copy-done, f32[257,1,128]{2,0,1:T(8,128)S(1)} %collective-permute-done, f32[257,34,1]{2,0,1:T(8,128)} %copy.29, f32[257,34,1]{2,0,1:T(8,128)} %copy.31, ...), kind=kLoop, calls=%fused_computation.23 | loop fusion | flops 28422144 | bytes 8803600 | tf_op jit(solution)/shard_map/mul | solution.py:53
  65.1 4.7 fusion.3
  70.1 4.2 fusion.64
  81.7 241.4 %all-reduce.4.cloned.1.call-done = f32[256,256]{0,1:T(8,128)} async-done(((f32[256,256]{0,1:T(8,128)}), f32[256,256]{0,1:T(8,128)}) %all-reduce.4.cloned.1.call-update) | async-done | bytes 262160 | tf_op jit(solution)/shard_map/psum | solution.py:29
  325.2 11.7 %cholesky.130 = f32[128,128]{1,0:T(8,128)S(1)} custom-call(f32[128,128]{1,0:T(8,128)S(1)} %cholesky.194), custom_call_target="Cholesky" | custom-call | tf_op jit(solution)/shard_map/jit(cholesky)/cholesky | solution.py:29
  336.9 9.8 %custom-call.21 = f32[1,128,128]{1,2,0:T(8,128)S(1)} custom-call(f32[1,128,128]{2,1,0:T(8,128)S(1)} %get-tuple-element.64), custom_call_target="InvertDiagBlocksLowerTriangular" | custom-call | tf_op jit(solution)/shard_map/jit(cholesky)/cholesky | solution.py:29
  347.3 11.7 %cholesky.147 = f32[128,128]{1,0:T(8,128)S(1)} custom-call(f32[128,128]{1,0:T(8,128)S(1)} %convolution_subtract_fusion.3), custom_call_target="Cholesky" | custom-call | tf_op jit(solution)/shard_map/jit(cholesky)/cholesky | solution.py:29
  361.7 4.0 while.2
  365.7 20.1 %custom-call.18 = f32[2,128,128]{1,2,0:T(8,128)S(1)} custom-call(f32[2,128,128]{2,1,0:T(8,128)S(1)} %get-tuple-element.11), custom_call_target="InvertDiagBlocksLowerTriangular" | custom-call | tf_op jit(solution)/shard_map/triangular_solve | solution.py:62
  398.5 5.6 copy.37
  413.4 78.3 %psum.23 = f32[256]{0:T(256)S(1)} all-reduce(f32[256]{0:T(256)S(1)} %bitcast.179), channel_id=1, replica_groups=mesh['band'=8,'tile'=32] {'band','tile'}, use_global_device_ids=true, to_apply=%region_6.8 | all-reduce | flops 256 | bytes 2048 | tf_op jit(solution)/shard_map/psum | solution.py:66
  492.0 4.8 maximum_multiply_fusion
  496.8 160.9 %all-reduce.6.cloned.1.call-done = f32[256,256]{1,0:T(8,128)} async-done(((f32[256,256]{1,0:T(8,128)}), f32[256,256]{1,0:T(8,128)}) %all-reduce.6.cloned.1.call-update) | async-done | bytes 262160 | tf_op jit(solution)/shard_map/psum | solution.py:66
  659.7 11.7 %cholesky.164 = f32[128,128]{1,0:T(8,128)S(1)} custom-call(f32[128,128]{1,0:T(8,128)S(1)} %cholesky.197), custom_call_target="Cholesky" | custom-call | tf_op jit(solution)/shard_map/jit(cholesky)/cholesky | solution.py:69
  671.4 9.8 %custom-call.22 = f32[1,128,128]{1,2,0:T(8,128)S(1)} custom-call(f32[1,128,128]{2,1,0:T(8,128)S(1)} %get-tuple-element.60), custom_call_target="InvertDiagBlocksLowerTriangular" | custom-call | tf_op jit(solution)/shard_map/jit(cholesky)/cholesky | solution.py:69
  681.7 11.7 %cholesky.181 = f32[128,128]{1,0:T(8,128)S(1)} custom-call(f32[128,128]{1,0:T(8,128)S(1)} %convolution_subtract_fusion.2), custom_call_target="Cholesky" | custom-call | tf_op jit(solution)/shard_map/jit(cholesky)/cholesky | solution.py:69
  696.1 4.0 while.3
  700.1 19.9 %custom-call.19 = f32[2,128,128]{1,2,0:T(8,128)S(1)} custom-call(f32[2,128,128]{2,1,0:T(8,128)S(1)} %get-tuple-element.19), custom_call_target="InvertDiagBlocksLowerTriangular" | custom-call | tf_op jit(solution)/shard_map/triangular_solve | solution.py:34
  723.2 3.7 fusion.60
  (109 shorter events, 68.0 us)
Async XLA Ops:
  7.2 4.7 copy-start.3
  7.2 315.9 %all-reduce.4.cloned.1.call-start = ((), (), s32[]{:S(2)}) async-start(), calls=%async_computation | async-start | bytes 524288 | tf_op jit(solution)/shard_map/psum | solution.py:29
  11.8 11.1 %copy-start = (f32[256,32,128]{2,0,1:T(8,128)}, f32[256,32,128]{2,0,1:T(8,128)S(1)}, u32[]{:S(2)}) copy-start(f32[256,32,128]{2,0,1:T(8,128)S(1)} %copy.27) | copy-start | bytes 12582916
  11.9 6.7 copy-start.8
  11.9 6.7 copy-start.5
  11.9 6.7 copy-start.6
  11.9 6.7 collective-permute-start
  16.6 6.3 collective-permute-start.1
  28.3 12.8 %copy-start.4 = (s32[32,128]{1,0:T(8,128)S(1)}, s32[32,128]{1,0:T(8,128)}, u32[]{:S(2)}) copy-start(s32[32,128]{1,0:T(8,128)} %param.13) | copy-start | bytes 49156
  31.9 9.2 %collective-permute-start.2 = (f32[257,34,1]{0,2,1:T(1,128)S(1)}, f32[257,34,1]{0,2,1:T(1,128)S(1)}, u32[]{:S(2)}, u32[]{:S(2)}) collective-permute-start(f32[257,34,1]{0,2,1:T(1,128)S(1)} %copy.28), channel_id=1, source_target_pairs={{1,0},{2,1},{3,2},{4,3},{5,4},{6,5},{7,6},{8,7},{9,8},{10,9},{11,1... | collective-permute-start | bytes 104864 | tf_op jit(solution)/shard_map/ppermute | solution.py:17
  36.8 7.1 collective-permute-start.3
  63.1 2.0 copy-start.1
  69.9 587.8 %all-reduce.6.cloned.1.call-start = ((), (), s32[]{:S(2)}) async-start(), calls=%async_computation.1 | async-start | bytes 524288 | tf_op jit(solution)/shard_map/psum | solution.py:66
  394.8 1.3 copy-start.2
  398.5 8.5 %copy-start.7 = (f32[1,1,64]{2,1,0:T(1,128)S(1)}, f32[1,1,64]{2,1,0:T(1,128)}, u32[]{:S(2)}) copy-start(f32[1,1,64]{2,1,0:T(1,128)} %param.16) | copy-start | bytes 772
  408.2 5.0 copy-start.9
Sparse Core Ops, SparseCore 0:
  70.0 253.0 all-reduce.3
  408.4 249.3 all-reduce.5
where the time goes:
time: 740 us; the launch traced here: 735 us
  waiting for transfers between devices  407 us (55%)
  other arithmetic  135 us (18%)
  blocking collectives  78.3 us (11%)
  local copies, waits for them, and re-layouts  61.1 us (8%)
  matrix products  24 us (3%)
  between operations  17.4 us (2%)
  starting transfers between devices  12.4 us (2%)
    psum x1, waiting for transfers between devices, factor_of(): return jnp.linalg.cholesky(lax.psum(gram, ('band', 'tile')))  241 us
    psum x1, waiting for transfers between devices, body(): c_total, b_total = lax.psum((local_c, local_b), ('band', 'tile'))  161 us
    psum x1, blocking collectives, body(): c_total, b_total = lax.psum((local_c, local_b), ('band', 'tile'))  78.3 us
    another operation x7, other arithmetic, factor_of(): return jnp.linalg.cholesky(lax.psum(gram, ('band', 'tile')))  34.6 us
    another operation x7, other arithmetic, body(): factor = jnp.linalg.cholesky(amat)  34.6 us
    another operation x4, other arithmetic, body(): lax.linalg.triangular_solve(lower, lmodes, left_side=True, lower=True)  22.5 us
    another operation x2, other arithmetic, chol_apply(): lax.linalg.triangular_solve(factor, half, left_side=True, lower=True, tra...  19.9 us
    mul x1, other arithmetic, body(): advanced = sea_mask.astype(jnp.float32) * (centre + tendency)  16.2 us
  transfers between devices with their start and end apart: 6, of which 3 were waited for; matrix products, arithmetic and copies ran while one was open for 4% of the time, Pallas kernels for 0%

commit v1 on v0

v1 whole, which is shorter than its diff:
```python
import jax
import jax.numpy as jnp
from jax import lax
from jax.sharding import PartitionSpec as P

HIGH = lax.Precision.HIGHEST
AXES = ("band", "tile")


def neighbours(block, axis, dim):
    count = lax.axis_size(axis)
    forward = [(i, i + 1) for i in range(count - 1)]
    backward = [(target, source) for source, target in forward]
    last = block.shape[dim] - 1
    low = lax.ppermute(lax.slice_in_dim(block, last, last + 1, axis=dim), axis, forward)
    high = lax.ppermute(lax.slice_in_dim(block, 0, 1, axis=dim), axis, backward)
    return low, high


def inner_rows(first, second):
    return lax.dot_general(
        first, second, (((1,), (1,)), ((), ())), precision=HIGH, preferred_element_type=jnp.float32
    )


def sum_everywhere(rows):
    mine = lax.all_to_all(rows, AXES, 0, 0, tiled=False).sum(0)
    return lax.all_to_all(jnp.broadcast_to(mine[None], rows.shape), AXES, 0, 0, tiled=False)


def body(mean_state, modes, east_vel, north_vel, sea_mask, obs_index, obs_value, obs_weight):
    count, lat_rows, lon_cols = modes.shape
    points = lat_rows * lon_cols
    fields = jnp.concatenate([mean_state[None], modes], axis=0)
    south, north = neighbours(fields, "band", 1)
    west, east = neighbours(fields, "tile", 2)
    northern = jnp.concatenate([fields[:, 1:], north], axis=1)
    southern = jnp.concatenate([south, fields[:, :-1]], axis=1)
    eastern = jnp.concatenate([fields[:, :, 1:], east], axis=2)
    western = jnp.concatenate([west, fields[:, :, :-1]], axis=2)
    tendency = -0.5 * east_vel * (eastern - western) - 0.5 * north_vel * (northern - southern)
    tendency = tendency + 0.2 * (eastern + western + northern + southern - 4.0 * fields)
    advanced = sea_mask.astype(jnp.float32) * (fields + tendency)
    mean_fore = advanced[0].reshape(points)
    lmodes = advanced[1:].reshape(count, points)
    indices = obs_index.reshape(-1)
    weights = obs_weight.reshape(-1)
    diff = obs_value.reshape(-1) - jnp.take(mean_fore, indices)
    gram = inner_rows(lmodes, lmodes)
    lobs = jnp.take(lmodes, indices, axis=1)
    obs_c = inner_rows(lobs * weights, lobs)
    obs_b = jnp.dot(lobs, weights * diff, precision=HIGH, preferred_element_type=jnp.float32)
    both = jnp.tril(gram) + jnp.triu(obs_c, 1)
    tail = jnp.stack([jnp.diagonal(obs_c), obs_b], axis=1)
    tail = jnp.pad(tail, ((0, 0), (0, 126)))
    packed = jnp.concatenate([both, tail], axis=1).reshape(count, 3, 128)
    total = sum_everywhere(packed).reshape(count, 384)
    both = total[:, :256]
    diag_c, b_total = total[:, 256], total[:, 257]
    low = jnp.tril(both, -1)
    gram = low + low.T + jnp.diag(jnp.diagonal(both))
    up = jnp.triu(both, 1)
    c_total = up + up.T + jnp.diag(diag_c)
    identity = jnp.eye(count, dtype=jnp.float32)
    amat = identity + c_total / (count - 1.0)
    lower, factor = jnp.linalg.cholesky(jnp.stack([gram, amat]))
    total_points = points * lax.axis_size("band") * lax.axis_size("tile")
    scale = jnp.sqrt(jnp.float32(total_points))
    linv = lax.linalg.triangular_solve(lower, identity, left_side=True, lower=True)
    right = jnp.concatenate([lower, b_total[:, None]], axis=1)
    half = lax.linalg.triangular_solve(factor, right, left_side=True, lower=True)
    root_factor = half[:, :count].T / scale
    solved = lax.linalg.triangular_solve(
        factor, half[:, count:], left_side=True, lower=True, transpose_a=True
    )[:, 0]
    increment = jnp.dot(solved / (count - 1.0), lmodes, precision=HIGH)
    mean_analysis = (mean_fore + increment).reshape(lat_rows, lon_cols)
    basis = jnp.dot(linv * scale, lmodes, precision=HIGH).reshape(count, lat_rows, lon_cols)
    return (mean_analysis, basis, root_factor)


def solution(mesh):
    return jax.shard_map(
        body,
        mesh=mesh,
        in_specs=(
            P("band", "tile"),
            P(None, "band", "tile"),
            P("band", "tile"),
            P("band", "tile"),
            P("band", "tile"),
            P("band", "tile", None),
            P("band", "tile", None),
            P("band", "tile", None),
        ),
        out_specs=(P("band", "tile"), P(None, "band", "tile"), P()),
        check_vma=False,
    )
```

time: 740 us -> 291 us (0.39)
  waiting for transfers between devices: 407 us -> 40 us
  blocking collectives: 78.3 us -> 0 us
  starting transfers between devices: 12.4 us -> 35.3 us
  between operations: 17.4 us -> 1.43 us
  local copies, waits for them, and re-layouts: 61.1 us -> 50.4 us
    psum x2 -> x0, waiting for transfers between devices: 402 us -> none  [the longest x1 241 us: factor_of(): return jnp.linalg.cholesky(lax.psum(gram, ('band', 'tile')))]
    psum x1 -> x0, blocking collectives: 78.3 us -> none  [body(): c_total, b_total = lax.psum((local_c, local_b), ('band', 'tile'))]
    all_to_all x0 -> x2, waiting for transfers between devices: none -> 39.9 us  [the longest x1 20 us: sum_everywhere(): mine = lax.all_to_all(rows, AXES, 0, 0, tiled=False).sum(0)]
    all_to_all x0 -> x2, starting transfers between devices: none -> 22 us  [the longest x1 15.3 us: sum_everywhere(): mine = lax.all_to_all(rows, AXES, 0, 0, tiled=False).sum(0)]
    another operation x22 -> x30, local copies, waits for them, and re-layouts: 23.5 us -> 8.9 us  [the longest x6 15.5 us: body(): lax.linalg.triangular_solve(lower, lmodes, left_side=True, lower=True)]
    concatenate x1 -> x4, other arithmetic: 0.02 us -> 13.2 us  [body(): fields = jnp.concatenate([mean_state[None], modes], axis=0)]
    mul x2 -> x1, other arithmetic: 21 us -> 12.2 us  [body(): advanced = sea_mask.astype(jnp.float32) * (fields + tendency)]
    another operation x16 -> x11, matrix products: 11.9 us -> 3.42 us  [the longest x3 1.11 us: body(): lax.linalg.triangular_solve(factor, right, left_side=True, lower=True)]
  transfers between devices with their start and end apart: 6 -> 6, of which waited for: 3 -> 2; matrix products, arithmetic and copies ran while one was open for 4% -> 6% of each run, Pallas kernels for 0% -> 0%
where the time goes in v1:
time: 291 us; the launch traced here: 287 us
  other arithmetic  134 us (46%)
  local copies, waits for them, and re-layouts  50.4 us (17%)
  waiting for transfers between devices  40 us (14%)
  starting transfers between devices  35.3 us (12%)
  matrix products  25 us (9%)
    another operation x13, other arithmetic, body(): lower, factor = jnp.linalg.cholesky(jnp.stack([gram, amat]))  67.4 us
    all_to_all x1, waiting for transfers between devices, sum_everywhere(): mine = lax.all_to_all(rows, AXES, 0, 0, tiled=False).sum(0)  20 us
    all_to_all x1, waiting for transfers between devices, sum_everywhere(): lax.all_to_all(jnp.broadcast_to(mine[None], rows.shape), AXES, 0, 0, tile...  19.9 us
    another operation x2, other arithmetic, body(): lax.linalg.triangular_solve(lower, identity, left_side=True, lower=True)  19.7 us
    another operation x3, other arithmetic, body(): lax.linalg.triangular_solve(factor, half[:, count:], left_side=True, lowe...  19.7 us
    all_to_all x1, starting transfers between devices, sum_everywhere(): mine = lax.all_to_all(rows, AXES, 0, 0, tiled=False).sum(0)  15.3 us
    concatenate x4, other arithmetic, body(): fields = jnp.concatenate([mean_state[None], modes], axis=0)  13.2 us
    mul x1, other arithmetic, body(): advanced = sea_mask.astype(jnp.float32) * (fields + tendency)  12.2 us
  transfers between devices with their start and end apart: 6, of which 2 were waited for; matrix products, arithmetic and copies ran while one was open for 6% of the time, Pallas kernels for 0%

profile of v1, /device:TPU:1, one launch (start us, length us, event | category | flops | bytes accessed | tf_op | source)
XLA Modules:
  0.0 286.6 jit_solution(16483609936444604310)
XLA Ops:
  0.6 4.6 %copy.59 = f32[256,32,128]{2,0,1:T(8,128)S(1)} copy(f32[256,32,128]{2,1,0:T(8,128)} %param.9) | data formatting | bytes 8388608 | tf_op args[1]
  5.3 4.5 %fusion.1 = (f32[257,32,1]{2,0,1:T(8,128)}, f32[257,32,1]{2,0,1:T(8,128)}) fusion(f32[1,32,128]{2,0,1:T(1,128)S(1)} %bitcast.165, f32[256,32,128]{2,0,1:T(8,128)S(1)} %copy.59), kind=kLoop, calls=%fused_computation.18 | loop fusion | flops 16448 | bytes 4276480 | tf_op jit(solution)/shard_map/concatenate | solution.py:34
  14.6 3.4 %copy.62 = f32[257,32,1]{0,1,2:T(8,128)S(1)} copy(f32[257,32,1]{2,0,1:T(8,128)} %get-tuple-element.88) | data formatting | bytes 65792 | tf_op jit(solution)/shard_map/slice | solution.py:15
  18.1 4.9 %collective-permute-start.1 = (f32[257,32,1]{0,1,2:T(8,128)S(1)}, f32[257,32,1]{0,1,2:T(8,128)S(1)}, u32[]{:S(2)}, u32[]{:S(2)}) collective-permute-start(f32[257,32,1]{0,1,2:T(8,128)S(1)} %copy.62), channel_id=1, source_target_pairs={{0,1},{1,2},{2,3},{3,4},{4,5},{5,6},{6,7},{7,8},{8,9},{9,10},{10,1... | collective-permute-start | bytes 98696 | tf_op jit(solution)/shard_map/ppermute | solution.py:15
  24.0 5.0 %collective-permute-start.2 = (f32[257,1,128]{2,0,1:T(8,128)S(1)}, f32[257,1,128]{2,0,1:T(8,128)S(1)}, u32[]{:S(2)}, u32[]{:S(2)}) collective-permute-start(f32[257,1,128]{2,0,1:T(8,128)S(1)} %get-tuple-element.91), channel_id=1, source_target_pairs={{32,0},{64,32},{96,64},{128,96},{160,128},{192,160},{224,192},{33,... | collective-permute-start | bytes 394760 | tf_op jit(solution)/shard_map/ppermute | solution.py:16
  31.2 4.1 %fusion = (f32[257,32,127]{2,0,1:T(8,128)}, f32[257,32,127]{2,0,1:T(8,128)}) fusion(f32[1,32,128]{2,0,1:T(1,128)S(1)} %bitcast.167, f32[256,32,128]{2,0,1:T(8,128)S(1)} %copy-done.1), kind=kLoop, calls=%fused_computation.17 | loop fusion | flops 2088896 | bytes 12566272 | tf_op jit(solution)/shard_map/concatenate | solution.py:34
  35.2 3.7 %fusion.6 = (f32[257,31,128]{2,0,1:T(8,128)}, f32[257,31,128]{2,0,1:T(8,128)}) fusion(f32[1,32,128]{2,0,1:T(1,128)S(1)} %bitcast.168, f32[256,32,128]{2,0,1:T(8,128)S(1)} %copy-done.1), kind=kLoop, calls=%fused_computation.28 | loop fusion | flops 2039552 | bytes 12368896 | tf_op jit(solution)/shard_map/concatenate | solution.py:34
  44.7 12.2 %add_multiply_fusion = f32[257,32,128]{2,0,1:T(8,128)S(1)} fusion(f32[1,32,128]{2,0,1:T(1,128)S(1)} %bitcast.169, f32[257,31,128]{2,0,1:T(8,128)} %get-tuple-element.90, f32[257,1,128]{2,0,1:T(8,128)S(1)} %collective-permute-done.3, f32[257,1,128]{2,0,1:T(8,128)S(1)} %collective-permute-done.2, f32[257,31,128]{2,0,1:T(8,128)} %get-tuple-element.89, ...), kind=kLoop, calls=%fused_computation.25 | loop fusion | flops 20000768 | bytes 25313280 | tf_op jit(solution)/shard_map/mul | solution.py:43
  60.3 5.7 %copy.64 = f32[256,32,128]{0,2,1:T(8,128)} copy(f32[256,32,128]{2,0,1:T(8,128)} %slice.170) | data formatting | bytes 8388608 | tf_op jit(solution)/shard_map/slice | solution.py:45
  69.4 11.7 %fusion.9 = f32[256,256]{0,1:T(8,128)S(1)} fusion(f32[256,256]{0,1:T(8,128)S(1)} %fusion.43, f32[257,32,128]{2,0,1:T(8,128)} %copy-done.3), kind=kOutput, calls=%fused_computation.34 | convolution fusion | flops 3221487616 | bytes 4718592 | tf_op jit(solution)/shard_map/dot_general | solution.py:21
  85.5 15.3 %all-to-all-start = ((f32[256,3,128]{2,1,0:T(4,128)}), f32[256,3,128]{2,1,0:T(4,128)S(1)}, u32[]{:S(2)}, u32[]{:S(2)}) async-start(f32[256,3,128]{2,1,0:T(4,128)} %copy.65), calls=%async_computation | async-start | bytes 1048576 | tf_op jit(solution)/shard_map/all_to_all | solution.py:27
  100.8 20.0 %all-to-all-done = f32[256,3,128]{2,1,0:T(4,128)S(1)} async-done(((f32[256,3,128]{2,1,0:T(4,128)}), f32[256,3,128]{2,1,0:T(4,128)S(1)}, u32[]{:S(2)}, u32[]{:S(2)}) %all-to-all-start) | async-done | bytes 393248 | tf_op jit(solution)/shard_map/all_to_all | solution.py:27
  122.0 6.7 %all-to-all-start.1 = ((f32[256,3,128]{2,1,0:T(4,128)}), f32[256,3,128]{2,1,0:T(4,128)S(1)}, u32[]{:S(2)}, u32[]{:S(2)}) async-start(f32[256,3,128]{2,1,0:T(4,128)} %broadcast_in_dim.80), calls=%async_computation.1 | async-start | bytes 1048576 | tf_op jit(solution)/shard_map/all_to_all | solution.py:28
  128.9 19.9 %all-to-all-done.1 = f32[256,3,128]{2,1,0:T(4,128)S(1)} async-done(((f32[256,3,128]{2,1,0:T(4,128)}), f32[256,3,128]{2,1,0:T(4,128)S(1)}, u32[]{:S(2)}, u32[]{:S(2)}) %all-to-all-start.1) | async-done | bytes 393248 | tf_op jit(solution)/shard_map/all_to_all | solution.py:28
  152.1 23.5 %custom-call.21 = f32[2,128,128]{2,1,0:T(8,128)S(1)} custom-call(f32[2,128,128]{2,1,0:T(8,128)S(1)} %cholesky.122), custom_call_target="Cholesky" | custom-call | tf_op jit(solution)/shard_map/jit(cholesky)/cholesky | solution.py:66
  175.7 19.7 %custom-call.22 = f32[2,1,128,128]{2,3,1,0:T(8,128)S(1)} custom-call(f32[2,1,128,128]{3,2,1,0:T(8,128)S(1)} %select_bitcast_fusion), custom_call_target="InvertDiagBlocksLowerTriangular" | custom-call | tf_op jit(solution)/shard_map/jit(cholesky)/cholesky | solution.py:66
  196.2 23.8 %custom-call.23 = f32[2,128,128]{2,1,0:T(8,128)S(1)} custom-call(f32[2,128,128]{2,1,0:T(8,128)S(1)} %convolution_subtract_fusion.2), custom_call_target="Cholesky" | custom-call | tf_op jit(solution)/shard_map/jit(cholesky)/cholesky | solution.py:66
  220.8 4.2 %while.2 = (s32[]{:T(128)}, f32[256,256]{0,1:T(8,128)S(1)}, s32[2,2]{1,0:T(2,128)S(1)}, f32[2,128,128]{2,1,0:T(8,128)S(1)}, s32[]{:T(128)}) while((s32[]{:T(128)}, f32[256,256]{0,1:T(8,128)S(1)}, s32[2,2]{1,0:T(2,128)S(1)}, f32[2,128,128]{2,1,0:T(8,128)S(1)}, s32[]{:T(128)}) %tuple.60), condition=%wide.while_cond, body=%wide.while_body.sunk | while | flops 2 | bytes 393321 | solution.py:73
  225.0 19.7 %custom-call.24 = f32[2,128,128]{1,2,0:T(8,128)S(1)} custom-call(f32[2,128,128]{2,1,0:T(8,128)S(1)} %get-tuple-element.10), custom_call_target="InvertDiagBlocksLowerTriangular" | custom-call | tf_op jit(solution)/shard_map/triangular_solve | solution.py:73
  246.8 4.2 %while.3 = (s32[]{:T(128)}, f32[256,256]{0,1:T(8,128)S(1)}, s32[2,2]{1,0:T(2,128)S(1)}, f32[2,128,128]{2,1,0:T(8,128)S(1)}, s32[]{:T(128)}) while((s32[]{:T(128)}, f32[256,256]{0,1:T(8,128)S(1)}, s32[2,2]{1,0:T(2,128)S(1)}, f32[2,128,128]{2,1,0:T(8,128)S(1)}, s32[]{:T(128)}) %tuple.66), condition=%wide.while_cond.1, body=%wide.while_body.1.sunk | while | flops 2 | bytes 393321 | solution.py:69
  251.1 19.7 %custom-call.25 = f32[2,128,128]{1,2,0:T(8,128)S(1)} custom-call(f32[2,128,128]{2,1,0:T(8,128)S(1)} %get-tuple-element.18), custom_call_target="InvertDiagBlocksLowerTriangular" | custom-call | tf_op jit(solution)/shard_map/triangular_solve | solution.py:69
  271.7 5.6 %fusion.4 = f32[256,32,128]{2,0,1:T(8,128)S(1)} fusion(f32[256,32,128]{0,2,1:T(8,128)} %copy.64, f32[128,256]{1,0:T(8,128)S(1)} %fusion.41, f32[128,256]{1,0:T(8,128)S(1)} %fusion.38), kind=kOutput, calls=%fused_computation.26 | convolution fusion | flops 3221356544 | bytes 8650752 | tf_op jit(solution)/shard_map/dot_general | solution.py:78
  277.4 4.4 %copy.79 = f32[256,32,128]{2,1,0:T(8,128)} copy(f32[256,32,128]{2,0,1:T(8,128)S(1)} %fusion.4) | data formatting | bytes 8388608
  282.3 3.5 %fusion.74 = f32[1,4096]{1,0:T(1,128)S(1)} fusion(f32[256,1]{0,1:T(1,128)S(1)} %bitcast.172, f32[256,4096]{0,1:T(8,128)S(1)} %bitcast.158), kind=kOutput, calls=%fused_computation.146 | convolution fusion | flops 12582912 | bytes 4211712 | tf_op jit(solution)/shard_map/dot_general | solution.py:76
  (118 shorter events, 43.3 us)
Async XLA Ops:
  0.6 4.7 %copy-start.4 = (f32[32,128]{1,0:T(8,128)S(1)}, f32[32,128]{1,0:T(8,128)}, u32[]{:S(2)}) copy-start(f32[32,128]{1,0:T(8,128)} %param.8) | copy-start | bytes 49156
  5.3 4.6 %copy-start = (f32[256,32,128]{2,0,1:T(8,128)}, f32[256,32,128]{2,0,1:T(8,128)S(1)}, u32[]{:S(2)}) copy-start(f32[256,32,128]{2,0,1:T(8,128)S(1)} %copy.59) | copy-start | bytes 12582916
  13.3 25.7 %collective-permute-start = (f32[257,32,1]{0,1,2:T(8,128)S(1)}, f32[257,32,1]{0,1,2:T(8,128)S(1)}, u32[]{:S(2)}, u32[]{:S(2)}) collective-permute-start(f32[257,32,1]{0,1,2:T(8,128)S(1)} %copy.60), channel_id=1, source_target_pairs={{1,0},{2,1},{3,2},{4,3},{5,4},{6,5},{7,6},{8,7},{9,8},{10,9},{11,1... | collective-permute-start | bytes 98696 | tf_op jit(solution)/shard_map/ppermute | solution.py:16
  18.1 13.1 %copy-start.1 = (f32[256,32,128]{2,0,1:T(8,128)S(1)}, f32[256,32,128]{2,0,1:T(8,128)}, u32[]{:S(2)}) copy-start(f32[256,32,128]{2,0,1:T(8,128)} %copy-done) | copy-start | bytes 12582916
  18.1 23.7 %collective-permute-start.1 = (f32[257,32,1]{0,1,2:T(8,128)S(1)}, f32[257,32,1]{0,1,2:T(8,128)S(1)}, u32[]{:S(2)}, u32[]{:S(2)}) collective-permute-start(f32[257,32,1]{0,1,2:T(8,128)S(1)} %copy.62), channel_id=1, source_target_pairs={{0,1},{1,2},{2,3},{3,4},{4,5},{5,6},{6,7},{7,8},{8,9},{9,10},{10,1... | collective-permute-start | bytes 98696 | tf_op jit(solution)/shard_map/ppermute | solution.py:15
  24.0 20.6 %collective-permute-start.2 = (f32[257,1,128]{2,0,1:T(8,128)S(1)}, f32[257,1,128]{2,0,1:T(8,128)S(1)}, u32[]{:S(2)}, u32[]{:S(2)}) collective-permute-start(f32[257,1,128]{2,0,1:T(8,128)S(1)} %get-tuple-element.91), channel_id=1, source_target_pairs={{32,0},{64,32},{96,64},{128,96},{160,128},{192,160},{224,192},{33,... | collective-permute-start | bytes 394760 | tf_op jit(solution)/shard_map/ppermute | solution.py:16
  29.1 15.6 %collective-permute-start.3 = (f32[257,1,128]{2,0,1:T(8,128)S(1)}, f32[257,1,128]{2,0,1:T(8,128)S(1)}, u32[]{:S(2)}, u32[]{:S(2)}) collective-permute-start(f32[257,1,128]{2,0,1:T(8,128)S(1)} %get-tuple-element.92), channel_id=1, source_target_pairs={{0,32},{32,64},{64,96},{96,128},{128,160},{160,192},{192,224},{1,3... | collective-permute-start | bytes 394760 | tf_op jit(solution)/shard_map/ppermute | solution.py:15
  35.2 3.7 %copy-start.9 = (s32[1,1,64]{2,1,0:T(1,128)S(1)}, s32[1,1,64]{2,1,0:T(1,128)}, u32[]{:S(2)}) copy-start(s32[1,1,64]{2,1,0:T(1,128)} %param.13) | copy-start | bytes 772
  35.2 3.7 %copy-start.6 = (f32[32,128]{1,0:T(8,128)S(1)}, f32[32,128]{1,0:T(8,128)}, u32[]{:S(2)}) copy-start(f32[32,128]{1,0:T(8,128)} %param.11) | copy-start | bytes 49156
  35.2 3.7 %copy-start.7 = (f32[32,128]{1,0:T(8,128)S(1)}, f32[32,128]{1,0:T(8,128)}, u32[]{:S(2)}) copy-start(f32[32,128]{1,0:T(8,128)} %param.10) | copy-start | bytes 49156
  35.2 3.8 %copy-start.5 = (s32[32,128]{1,0:T(8,128)S(1)}, s32[32,128]{1,0:T(8,128)}, u32[]{:S(2)}) copy-start(s32[32,128]{1,0:T(8,128)} %param.12) | copy-start | bytes 49156
  56.9 3.4 %copy-start.3 = (f32[257,32,128]{2,0,1:T(8,128)}, f32[257,32,128]{2,0,1:T(8,128)S(1)}, u32[]{:S(2)}) copy-start(f32[257,32,128]{2,0,1:T(8,128)S(1)} %add_multiply_fusion) | copy-start | bytes 12632068
  60.3 8.6 %copy-start.8 = (f32[1,1,64]{2,1,0:T(1,128)S(1)}, f32[1,1,64]{2,1,0:T(1,128)}, u32[]{:S(2)}) copy-start(f32[1,1,64]{2,1,0:T(1,128)} %param.15) | copy-start | bytes 772
  66.0 18.3 %copy-start.10 = (f32[1,1,64]{2,1,0:T(1,128)S(1)}, f32[1,1,64]{2,1,0:T(1,128)}, u32[]{:S(2)}) copy-start(f32[1,1,64]{2,1,0:T(1,128)} %param.14) | copy-start | bytes 772
  85.5 35.3 %all-to-all-start = ((f32[256,3,128]{2,1,0:T(4,128)}), f32[256,3,128]{2,1,0:T(4,128)S(1)}, u32[]{:S(2)}, u32[]{:S(2)}) async-start(f32[256,3,128]{2,1,0:T(4,128)} %copy.65), calls=%async_computation | async-start | bytes 1048576 | tf_op jit(solution)/shard_map/all_to_all | solution.py:27
  122.0 26.8 %all-to-all-start.1 = ((f32[256,3,128]{2,1,0:T(4,128)}), f32[256,3,128]{2,1,0:T(4,128)S(1)}, u32[]{:S(2)}, u32[]{:S(2)}) async-start(f32[256,3,128]{2,1,0:T(4,128)} %broadcast_in_dim.80), calls=%async_computation.1 | async-start | bytes 1048576 | tf_op jit(solution)/shard_map/all_to_all | solution.py:28
  277.4 4.9 %copy-start.2 = (f32[256,32,128]{0,2,1:T(8,128)S(1)}, f32[256,32,128]{0,2,1:T(8,128)}, u32[]{:S(2)}) copy-start(f32[256,32,128]{0,2,1:T(8,128)} %copy.64) | copy-start | bytes 12582916

commit v2 on v0

v2 whole, which is shorter than its diff:
```python
import functools

import jax
import jax.numpy as jnp
from jax import lax
from jax.experimental import pallas as pl
from jax.experimental.pallas import tpu as pltpu
from jax.sharding import PartitionSpec as P

HIGH = lax.Precision.HIGHEST
PANEL = 16
LANES = 128
PACK = 576
VMEM = pl.BlockSpec(memory_space=pltpu.VMEM)
SMEM = pl.BlockSpec(memory_space=pltpu.SMEM)
ROOM = pltpu.CompilerParams(vmem_limit_bytes=48 * 2**20)


def high_dot(a, b, dims):
    return lax.dot_general(
        a, b, (dims, ((), ())), precision=HIGH, preferred_element_type=jnp.float32
    )


def lanes_of(shape):
    return lax.broadcasted_iota(jnp.int32, shape, len(shape) - 1)


def edges_kernel(groups, modes_ref, mean_ref, slab_ref, low_ref, high_ref, west_ref, east_ref):
    step = pl.program_id(0)
    rows, lats = modes_ref.shape[0], modes_ref.shape[1]
    total = rows * groups
    lane = lanes_of((rows, LANES))
    west = jnp.zeros((rows, LANES), jnp.float32)
    east = jnp.zeros((rows, LANES), jnp.float32)
    here = pl.ds(pl.multiple_of(step * rows, rows), rows)
    for lat in range(lats):
        slab = modes_ref[:, lat, :]
        slab_ref[lat] = slab
        turned = pltpu.roll(slab, lat + 1, 1)
        west = jnp.where(lane == lat + 1, turned, west)
        east = jnp.where(lane == lat, turned, east)
        if lat == 0:
            low_ref[here] = slab
        if lat == lats - 1:
            high_ref[here] = slab
    base = step * lats
    west = pltpu.roll(west, base, 1)
    east = pltpu.roll(east, base, 1)
    from_base = lanes_of((rows, LANES)) - base
    east_here = (from_base >= 0) & (from_base < lats)
    shifted = lax.rem(from_base + LANES - 1, LANES)
    west_here = (shifted >= 0) & (shifted < lats)
    east_ref[0:rows] = jnp.where(east_here, east, east_ref[0:rows])
    west_ref[0:rows] = jnp.where(west_here, west, west_ref[0:rows])

    @pl.when(step == 0)
    def _():
        west_ref[rows : rows + lats] = mean_ref[...]
        east_ref[rows : rows + lats] = mean_ref[...]
        low_ref[total : total + 8] = jnp.broadcast_to(mean_ref[0:1], (8, LANES))
        high_ref[total : total + 8] = jnp.broadcast_to(mean_ref[lats - 1 : lats], (8, LANES))


def edges_of(modes, mean_state):
    count, lats, lons = modes.shape
    groups = lons // lats
    rows = count // groups
    whole = lambda shape: pl.BlockSpec(shape, lambda i: (0,) * len(shape))
    sides = [(count + 8, lons), (count + 8, lons), (rows + lats, lons), (rows + lats, lons)]
    return pl.pallas_call(
        functools.partial(edges_kernel, groups),
        grid=(groups,),
        in_specs=[pl.BlockSpec((rows, lats, lons), lambda i: (i, 0, 0)), whole((lats, lons))],
        out_specs=[pl.BlockSpec((lats, rows, lons), lambda i: (0, i, 0))] + [whole(s) for s in sides],
        out_shape=[jax.ShapeDtypeStruct((lats, count, lons), jnp.float32)]
        + [jax.ShapeDtypeStruct(s, jnp.float32) for s in sides],
        compiler_params=ROOM,
        name="edges",
    )(modes, mean_state)


def split(value):
    top = value.astype(jnp.bfloat16)
    return top, (value - top.astype(jnp.float32)).astype(jnp.bfloat16)


def pair_rows(a, b):
    return lax.dot_general(a, b, (((1,), (1,)), ((), ())), preferred_element_type=jnp.float32)


def sums_kernel(
    slab_ref, mean_ref, north_ref, south_ref, east_ref, west_ref, uvel_ref, vvel_ref, mask_ref,
    index_ref, value_ref, weight_ref, adv_ref, fore_ref, pack_ref, coef, parts, seen, seen_mean,
):
    lats, count, lons = slab_ref.shape
    groups = lons // lats
    rows = count // groups
    sea = mask_ref[...].astype(jnp.float32)
    half_u, half_v = 0.5 * uvel_ref[...], 0.5 * vvel_ref[...]
    coef[0] = sea * 0.2
    coef[1] = sea * (0.2 - half_u)
    coef[2] = sea * (0.2 + half_u)
    coef[3] = sea * (0.2 - half_v)
    coef[4] = sea * (0.2 + half_v)
    first = lanes_of((lats, lons)) == 0
    last = lanes_of((lats, lons)) == lons - 1
    mean = mean_ref[...]
    eastern = jnp.where(last, east_ref[rows : rows + lats, 0:1], pltpu.roll(mean, lons - 1, 1))
    western = jnp.where(first, west_ref[rows : rows + lats, lons - 1 : lons], pltpu.roll(mean, 1, 1))
    northern = jnp.concatenate([mean[1:], north_ref[count : count + 1]], axis=0)
    southern = jnp.concatenate([south_ref[count : count + 1], mean[:-1]], axis=0)
    fore = coef[0] * mean + coef[1] * eastern + coef[2] * western
    fore_ref[...] = fore + coef[3] * northern + coef[4] * southern

    first = lanes_of((rows, lons)) == 0
    last = lanes_of((rows, lons)) == lons - 1

    def advance(lat, northern, southern):
        factors = [coef[i, pl.ds(lat, 1), :] for i in range(5)]
        out = []
        for g in range(groups):
            span = slice(g * rows, (g + 1) * rows)
            centre = slab_ref[lat, span, :]
            east_edge = pltpu.roll(east_ref[0:rows], lax.rem(3 * lons - 2 - g * lats - lat, lons), 1)
            west_edge = pltpu.roll(west_ref[0:rows], lax.rem(2 * lons - g * lats - lat, lons), 1)
            eastern = jnp.where(last, east_edge, pltpu.roll(centre, lons - 1, 1))
            western = jnp.where(first, west_edge, pltpu.roll(centre, 1, 1))
            moved = factors[0] * centre + factors[1] * eastern + factors[2] * western
            moved = moved + factors[3] * northern[span, :] + factors[4] * southern[span, :]
            adv_ref[lat, span, :] = moved
            out.append(moved)
        return jnp.concatenate(out, axis=0)

    def add(lat, one, two):
        top, low = split(jnp.concatenate([one, two], axis=1))
        parts[0] += pair_rows(top, top) + pair_rows(low, low)
        parts[1] += pair_rows(top, low)

    parts[...] = jnp.zeros_like(parts)
    add(0, advance(0, slab_ref.at[1], south_ref), advance(1, slab_ref.at[2], slab_ref.at[0]))

    def middle(i, carry):
        lat = 2 * i
        one = advance(lat, slab_ref.at[lat + 1], slab_ref.at[lat - 1])
        two = advance(lat + 1, slab_ref.at[lat + 2], slab_ref.at[lat])
        add(lat, one, two)
        return carry

    lax.fori_loop(1, lats // 2 - 1, middle, 0)
    end = lats - 1
    add(
        end - 1,
        advance(end - 1, slab_ref.at[end], slab_ref.at[end - 2]),
        advance(end, north_ref, slab_ref.at[end - 1]),
    )

    observed = index_ref.shape[-1]
    seen[...] = jnp.zeros_like(seen)
    seen_mean[...] = jnp.zeros_like(seen_mean)
    lane = lanes_of((count, lons))

    def look(k, carry):
        point = index_ref[0, 0, k]
        lat, lon = point // lons, lax.rem(point, lons)
        turn = lax.rem(k + lons - lon, lons)
        column = pltpu.roll(adv_ref[lat], turn, 1)
        seen[...] = jnp.where(lane == k, column, seen[...])
        line = pltpu.roll(jnp.broadcast_to(fore_ref[pl.ds(lat, 1), :], (8, lons)), turn, 1)
        seen_mean[...] = jnp.where(lane[0:8] == k, line, seen_mean[...])
        return carry

    lax.fori_loop(0, observed, look, 0)
    used = lanes_of((1, lons)) < observed
    weights = jnp.where(used, weight_ref[...], 0.0)
    diff = value_ref[...] - seen_mean[0:1]
    found = seen[...]
    obs_c = high_dot(found * weights, found, ((1,), (1,)))
    obs_b = high_dot(jnp.broadcast_to(weights * diff, (8, lons)), found, ((1,), (1,)))
    cross = parts[1]
    gram = parts[0] + (cross + cross.T)
    row = lax.broadcasted_iota(jnp.int32, (count, count), 0)
    col = lax.broadcasted_iota(jnp.int32, (count, count), 1)
    both = jnp.where(row >= col, gram, obs_c)
    diag_c = jnp.sum(jnp.where(row == col, obs_c, 0.0), axis=0, keepdims=True)
    pack_ref[0:count] = both[:, 0:lons]
    pack_ref[count : 2 * count] = both[:, lons:]
    pack_ref[2 * count :] = jnp.zeros((PACK - 2 * count, lons), jnp.float32)
    for i, line in enumerate((diag_c, obs_b[0:1])):
        pack_ref[2 * count + 2 * i : 2 * count + 2 * i + 1] = line[:, 0:lons]
        pack_ref[2 * count + 2 * i + 1 : 2 * count + 2 * i + 2] = line[:, lons:]


def sums_of(slabs, mean_state, sides, east_vel, north_vel, sea_mask, obs_index, obs_value, obs_weight):
    lats, count, lons = slabs.shape
    pad = lambda x: jnp.pad(x.reshape(1, -1), ((0, 0), (0, lons - x.size)))
    return pl.pallas_call(
        sums_kernel,
        in_specs=[VMEM] * 9 + [SMEM] + [VMEM] * 2,
        out_specs=[VMEM] * 3,
        out_shape=[
            jax.ShapeDtypeStruct((lats, count, lons), jnp.float32),
            jax.ShapeDtypeStruct((lats, lons), jnp.float32),
            jax.ShapeDtypeStruct((PACK, lons), jnp.float32),
        ],
        scratch_shapes=[
            pltpu.VMEM((5, lats, lons), jnp.float32),
            pltpu.VMEM((2, count, count), jnp.float32),
            pltpu.VMEM((count, lons), jnp.float32),
            pltpu.VMEM((8, lons), jnp.float32),
        ],
        compiler_params=ROOM,
        name="sums",
    )(slabs, mean_state, *sides, east_vel, north_vel, sea_mask, obs_index, pad(obs_value), pad(obs_weight))


def exchange(value, axis, mask):
    return lax.ppermute(value, axis, [(i, i ^ mask) for i in range(lax.axis_size(axis))])


HALVING = (("band", 1, (0,)), ("band", 2, (1, 2)), ("band", 6, (2,)))
DOUBLING = (("tile", 1), ("tile", 3), ("tile", 4), ("tile", 8), ("tile", 24))


def sum_everywhere(value):
    uppers = []
    for axis, mask, bits in HALVING:
        half = value.shape[0] // 2
        low, high = value[:half], value[half:]
        upper = sum(lax.axis_index(axis) >> bit for bit in bits) & 1 == 1
        uppers.append(upper)
        value = jnp.where(upper, high, low) + exchange(jnp.where(upper, low, high), axis, mask)
    for axis, mask in DOUBLING:
        value = value + exchange(value, axis, mask)
    for (axis, mask, _), upper in zip(HALVING[::-1], uppers[::-1]):
        other = exchange(value, axis, mask)
        value = jnp.concatenate([jnp.where(upper, other, value), jnp.where(upper, value, other)])
    return value


def factor_panels(work, upper, inverse):
    size = work.shape[1]
    tiles = size // LANES
    lane = lanes_of((PANEL, LANES))
    sub = lax.broadcasted_iota(jnp.int32, (PANEL, LANES), 0)
    lane_row = lanes_of((1, LANES))
    for first in range(0, size, PANEL):
        home, at = first // LANES, first % LANES
        inside = (lane >= at) & (lane < at + PANEL)
        state = []
        for m in range(2):
            rows = [work[m, first : first + PANEL, t * LANES : (t + 1) * LANES] for t in range(tiles)]
            cols = [
                jnp.broadcast_to(rows[home][:, at + k : at + k + 1], (PANEL, LANES))
                for k in range(PANEL)
            ]
            block = jnp.where(inside, rows[home], 0.0)
            rows[home] = jnp.where(inside, jnp.where(lane == sub + at, 1.0, 0.0), rows[home])
            state.append((rows + [block], cols))
        for j in range(0, PANEL, 2):
            pair = (sub == j) | (sub == j + 1)
            for m in range(2):
                rows, cols = state[m]
                c0, c1 = cols[j], cols[j + 1]
                a, b, d = c0[j : j + 1], c1[j : j + 1], c1[j + 1 : j + 2]
                rdet = 1.0 / (a * d - b * b)
                i00, i01, i11 = d * rdet, -b * rdet, a * rdet
                m0 = c0 * i00 + c1 * i01
                m1 = c0 * i01 + c1 * i11
                m0 = jnp.where(sub == j, -i00, jnp.where(sub == j + 1, -i01, m0))
                m1 = jnp.where(sub == j, -i01, jnp.where(sub == j + 1, -i11, m1))
                for k in range(j + 2, PANEL):
                    ck = cols[k]
                    cols[k] = jnp.where(pair, 0.0, ck) - m0 * ck[j : j + 1] - m1 * ck[j + 1 : j + 2]
                ra = lax.rsqrt(a)
                ra = ra * (1.5 - 0.5 * a * ra * ra)
                ratio = b * ra * ra
                rest = d - ratio * b
                rb = lax.rsqrt(rest)
                rb = rb * (1.5 - 0.5 * rest * rb * rb)
                for t in range(tiles + 1):
                    r0, r1 = rows[t][j : j + 1], rows[t][j + 1 : j + 2]
                    done = (r0 * ra, (r1 - ratio * r0) * rb)
                    rows[t] = jnp.where(pair, 0.0, rows[t]) - m0 * r0 - m1 * r1
                    if t == tiles:
                        extra = done
                    elif t == home:
                        mine = done
                    else:
                        target, other = (inverse, upper) if t < home else (upper, inverse)
                        span = slice(t * LANES, (t + 1) * LANES)
                        target[m, first + j : first + j + 1, span] = done[0]
                        target[m, first + j + 1 : first + j + 2, span] = done[1]
                        other[m, first + j : first + j + 2, span] = jnp.zeros((2, LANES), jnp.float32)
                span = slice(home * LANES, (home + 1) * LANES)
                for e in range(2):
                    row = slice(first + j + e, first + j + e + 1)
                    left = lane_row < at + PANEL
                    inverse[m, row, span] = jnp.where(left, mine[e], 0.0)
                    corner = jnp.where(lane_row >= at + j + e, extra[e], 0.0)
                    upper[m, row, span] = jnp.where(left, corner, mine[e])
        for m in range(2):
            panel = jnp.concatenate(state[m][0][:tiles], axis=1)
            blocks = [panel]
            if at:
                blocks.insert(0, jnp.zeros((at, size), jnp.float32))
            if at + PANEL < LANES:
                blocks.append(jnp.zeros((LANES - at - PANEL, size), jnp.float32))
            panel = jnp.concatenate(blocks, axis=0)
            for start, stop in ((first + PANEL, first + 2 * PANEL), (first + 2 * PANEL, size)):
                if start >= min(stop, size):
                    continue
                left = work[m, start:stop, home * LANES : (home + 1) * LANES]
                change = high_dot(left, panel, ((1,), (0,)))
                place = lanes_of(left.shape)
                for t in range(tiles):
                    span = slice(t * LANES, (t + 1) * LANES)
                    if t == home:
                        old = jnp.where((place >= at) & (place < at + PANEL), 0.0, left)
                    else:
                        old = work[m, start:stop, span]
                    work[m, start:stop, span] = old - change[:, span]


def factor_kernel(scale, pack_ref, linv_ref, coef_ref, root_ref, work, upper, inverse):
    size = linv_ref.shape[0]
    row = lax.broadcasted_iota(jnp.int32, (size, size), 0)
    col = lax.broadcasted_iota(jnp.int32, (size, size), 1)
    eye = row == col
    both = jnp.concatenate([pack_ref[0:size], pack_ref[size : 2 * size]], axis=1)
    turned = both.T
    line = lambda i: jnp.concatenate(
        [pack_ref[2 * size + i : 2 * size + i + 1], pack_ref[2 * size + i + 1 : 2 * size + i + 2]], axis=1
    )
    gram = jnp.where(row >= col, both, turned)
    obs_c = jnp.where(row < col, both, jnp.where(eye, line(0), turned))
    only = jnp.where(eye, both, 0.0)
    q_row = lax.rsqrt(jnp.sum(only, axis=0, keepdims=True))
    work[0] = gram * q_row * lax.rsqrt(jnp.sum(only, axis=1, keepdims=True))
    work[1] = jnp.where(eye, 1.0, 0.0) + obs_c / (size - 1.0)
    factor_panels(work, upper, inverse)
    linv_ref[...] = inverse[0] * (q_row * scale)
    finv = inverse[1]
    root_ref[...] = high_dot(upper[0] * ((1.0 / q_row) / scale), finv, ((1,), (1,)))
    half = high_dot(jnp.broadcast_to(line(2), (8, size)), finv, ((1,), (1,)))
    coef_ref[...] = high_dot(half, finv, ((1,), (0,))) / (size - 1.0)


def factor_all(pack, size, scale):
    full = jax.ShapeDtypeStruct((size, size), jnp.float32)
    return pl.pallas_call(
        functools.partial(factor_kernel, scale),
        in_specs=[VMEM],
        out_specs=[VMEM] * 3,
        out_shape=(full, jax.ShapeDtypeStruct((8, size), jnp.float32), full),
        scratch_shapes=[pltpu.VMEM((2, size, size), jnp.float32)] * 3,
        compiler_params=ROOM,
        name="factors",
    )(pack)


def apply_kernel(adv_ref, linv_ref, coef_ref, fore_ref, basis_ref, mean_ref):
    lats = adv_ref.shape[0]
    count = linv_ref.shape[0]
    left = jnp.concatenate([linv_ref[...], coef_ref[...]], axis=0)
    for lat in range(0, lats, 2):
        pair = jnp.concatenate([adv_ref[lat], adv_ref[lat + 1]], axis=1)
        out = high_dot(left, pair, ((1,), (0,)))
        for e in range(2):
            part = out[:, e * LANES : (e + 1) * LANES]
            basis_ref[:, lat + e, :] = part[0:count]
            mean_ref[lat + e : lat + e + 1] = fore_ref[lat + e : lat + e + 1] + part[count : count + 1]


def apply_all(advanced, linv, coef, fore):
    lats, count, lons = advanced.shape
    step = 8
    whole = lambda shape: pl.BlockSpec(shape, lambda i: (0,) * len(shape))
    return pl.pallas_call(
        apply_kernel,
        grid=(lats // step,),
        in_specs=[
            pl.BlockSpec((step, count, lons), lambda i: (i, 0, 0)),
            whole(linv.shape),
            whole(coef.shape),
            pl.BlockSpec((step, lons), lambda i: (i, 0)),
        ],
        out_specs=[
            pl.BlockSpec((count, step, lons), lambda i: (0, i, 0)),
            pl.BlockSpec((step, lons), lambda i: (i, 0)),
        ],
        out_shape=[
            jax.ShapeDtypeStruct((count, lats, lons), jnp.float32),
            jax.ShapeDtypeStruct((lats, lons), jnp.float32),
        ],
        compiler_params=ROOM,
        name="apply",
    )(advanced, linv, coef, fore)


def body(mean_state, modes, east_vel, north_vel, sea_mask, obs_index, obs_value, obs_weight):
    count, lat_rows, lon_cols = modes.shape
    slabs, low, high, west, east = edges_of(modes, mean_state)
    up = lambda axis: [(i, i + 1) for i in range(lax.axis_size(axis) - 1)]
    down = lambda axis: [(j, i) for i, j in up(axis)]
    from_north = lax.ppermute(low, "band", down("band"))
    from_south = lax.ppermute(high, "band", up("band"))
    from_east = lax.ppermute(west, "tile", down("tile"))
    from_west = lax.ppermute(east, "tile", up("tile"))
    sides = (from_north, from_south, from_east, from_west)
    advanced, fore, pack = sums_of(
        slabs, mean_state, sides, east_vel, north_vel, sea_mask, obs_index, obs_value, obs_weight
    )
    pack = sum_everywhere(pack)
    points = lat_rows * lon_cols * lax.axis_size("band") * lax.axis_size("tile")
    linv, coef, root_factor = factor_all(pack, count, float(points) ** 0.5)
    basis, mean_analysis = apply_all(advanced, linv, coef, fore)
    return (mean_analysis, basis, root_factor)


def solution(mesh):
    return jax.shard_map(
        body,
        mesh=mesh,
        in_specs=(
            P("band", "tile"),
            P(None, "band", "tile"),
            P("band", "tile"),
            P("band", "tile"),
            P("band", "tile"),
            P("band", "tile", None),
            P("band", "tile", None),
            P("band", "tile", None),
        ),
        out_specs=(P("band", "tile"), P(None, "band", "tile"), P()),
        check_vma=False,
    )
```

time: 740 us -> 121 us (0.16)
  waiting for transfers between devices: 407 us -> 21.7 us
  other arithmetic: 135 us -> 0.2 us
  blocking collectives: 78.3 us -> 0 us
  local copies, waits for them, and re-layouts: 61.1 us -> 6.95 us
  Pallas kernels: 0 us -> 44.3 us
  starting transfers between devices: 12.4 us -> 46.2 us
  matrix products: 24 us -> 0 us
  between operations: 17.4 us -> 0.91 us
    psum x2 -> x0, waiting for transfers between devices: 402 us -> none  [the longest x1 241 us: factor_of(): return jnp.linalg.cholesky(lax.psum(gram, ('band', 'tile')))]
    another operation x20 -> x0, other arithmetic: 112 us -> none  [the longest x7 34.6 us: factor_of(): return jnp.linalg.cholesky(lax.psum(gram, ('band', 'tile')))]
    psum x1 -> x0, blocking collectives: 78.3 us -> none  [body(): c_total, b_total = lax.psum((local_c, local_b), ('band', 'tile'))]
    pallas_call x0 -> x4, Pallas kernels: none -> 44.3 us  [the longest x1 19.6 us: sums_of(): pl.pallas_call(sums_kernel, in_specs=[VMEM] * 9 + [SMEM] + [VMEM] * 2, ou...]
    ppermute x4 -> x15, starting transfers between devices: 12.1 us -> 46.2 us  [the longest x11 33.9 us: exchange(): lax.ppermute(value, axis, [(i, i ^ mask) for i in range(lax.axis_size(axi...]
    another operation x22 -> x0, local copies, waits for them, and re-layouts: 23.5 us -> none  [the longest x6 15.5 us: body(): lax.linalg.triangular_solve(lower, lmodes, left_side=True, lower=True)]
    mul x3 -> x0, other arithmetic: 21 us -> none  [the longest x1 16.2 us: body(): advanced = sea_mask.astype(jnp.float32) * (centre + tendency)]
    ppermute x4 -> x15, waiting for transfers between devices: 4.3 us -> 21.7 us  [the longest x11 20.6 us: exchange(): lax.ppermute(value, axis, [(i, i ^ mask) for i in range(lax.axis_size(axi...]
  transfers between devices with their start and end apart: 6 -> 15, of which waited for: 3 -> 12; matrix products, arithmetic and copies ran while one was open for 4% -> 0% of each run, Pallas kernels for 0% -> 0%
where the time goes in v2:
time: 121 us; the launch traced here: 120 us
  starting transfers between devices  46.2 us (38%)
  Pallas kernels  44.3 us (37%)
  waiting for transfers between devices  21.7 us (18%)
  local copies, waits for them, and re-layouts  6.95 us (6%)
    ppermute x11, starting transfers between devices, exchange(): lax.ppermute(value, axis, [(i, i ^ mask) for i in range(lax.axis_size(axi...  33.9 us
    ppermute x11, waiting for transfers between devices, exchange(): lax.ppermute(value, axis, [(i, i ^ mask) for i in range(lax.axis_size(axi...  20.6 us
    pallas_call x1, Pallas kernels, sums_of(): pl.pallas_call(sums_kernel, in_specs=[VMEM] * 9 + [SMEM] + [VMEM] * 2, ou...  19.6 us
    pallas_call x1, Pallas kernels, factor_all(): pl.pallas_call(functools.partial(factor_kernel, scale), in_specs=[VMEM],...  11.7 us
    pallas_call x1, Pallas kernels, apply_all(): pl.pallas_call(apply_kernel, grid=(lats // step,), in_specs=[pl.BlockSpec...  7.19 us
    unnamed x22, local copies, waits for them, and re-layouts  6.94 us
    pallas_call x1, Pallas kernels, edges_of(): pl.pallas_call(functools.partial(edges_kernel, groups), grid=(groups,), i...  5.74 us
    ppermute x1, starting transfers between devices, body(): from_north = lax.ppermute(low, 'band', down('band'))  5.14 us
  transfers between devices with their start and end apart: 15, of which 12 were waited for; matrix products, arithmetic and copies ran while one was open for 0% of the time, Pallas kernels for 0%

profile of v2, /device:TPU:1, one launch (start us, length us, event | category | flops | bytes accessed | tf_op | source)
XLA Modules:
  0.0 120.3 jit_solution(16010963623748970867)
XLA Ops:
  1.4 5.7 %edges.1 = (f32[32,256,128]{2,1,0:T(8,128)S(1)}, f32[264,128]{1,0:T(8,128)S(1)}, f32[264,128]{1,0:T(8,128)S(1)}, f32[96,128]{1,0:T(8,128)S(1)}, f32[96,128]{1,0:T(8,128)S(1)}) custom-call(f32[256,32,128]{2,1,0:T(8,128)} %modes_ref.1, f32[32,128]{1,0:T(8,128)S(1)} %copy-done.3), custom_call_target="tpu_custom_call" | custom-call | tf_op jit(solution)/shard_map/edges/pallas_call | solution.py:71
  7.2 2.0 %copy-done.2 = f32[32,256,128]{2,1,0:T(8,128)} copy-done((f32[32,256,128]{2,1,0:T(8,128)}, f32[32,256,128]{2,1,0:T(8,128)S(1)}, u32[]{:S(2)}) %copy-start.2) | copy-done | bytes 4194328
  9.2 5.1 %collective-permute-start = (f32[264,128]{1,0:T(8,128)S(1)}, f32[264,128]{1,0:T(8,128)S(1)}, u32[]{:S(2)}, u32[]{:S(2)}) collective-permute-start(f32[264,128]{1,0:T(8,128)S(1)} %get-tuple-element.17), channel_id=1, source_target_pairs={{32,0},{64,32},{96,64},{128,96},{160,128},{192,160},{224,192},{33,... | collective-permute-start | bytes 405512 | tf_op jit(solution)/shard_map/ppermute | solution.py:406
  14.3 1.9 %collective-permute-start.1 = (f32[264,128]{1,0:T(8,128)S(1)}, f32[264,128]{1,0:T(8,128)S(1)}, u32[]{:S(2)}, u32[]{:S(2)}) collective-permute-start(f32[264,128]{1,0:T(8,128)S(1)} %get-tuple-element.18), channel_id=1, source_target_pairs={{0,32},{32,64},{64,96},{96,128},{128,160},{160,192},{192,224},{1,3... | collective-permute-start | bytes 405512 | tf_op jit(solution)/shard_map/ppermute | solution.py:407
  17.5 4.0 %collective-permute-start.3 = (f32[96,128]{1,0:T(8,128)S(1)}, f32[96,128]{1,0:T(8,128)S(1)}, u32[]{:S(2)}, u32[]{:S(2)}) collective-permute-start(f32[96,128]{1,0:T(8,128)S(1)} %get-tuple-element.20), channel_id=1, source_target_pairs={{0,1},{1,2},{2,3},{3,4},{4,5},{5,6},{6,7},{7,8},{8,9},{9,10},{10,1... | collective-permute-start | bytes 147464 | tf_op jit(solution)/shard_map/ppermute | solution.py:409
  22.7 19.6 %sums.1 = (f32[32,256,128]{2,1,0:T(8,128)S(1)}, f32[32,128]{1,0:T(8,128)S(1)}, f32[576,128]{1,0:T(8,128)S(1)}) custom-call(f32[32,256,128]{2,1,0:T(8,128)} %copy-done.2, f32[32,128]{1,0:T(8,128)S(1)} %copy-done.4, f32[264,128]{1,0:T(8,128)S(1)} %collective-permute-done.north_ref, f32[264,128]{1,0:T(8,128)S(1)} %collective-permute-done.1.south_ref, ...), custom_call_target="tpu_custom_call" | custom-call | tf_op jit(solution)/shard_map/sums/pallas_call | solution.py:197
  42.4 2.0 %copy-done = f32[32,256,128]{2,1,0:T(8,128)} copy-done((f32[32,256,128]{2,1,0:T(8,128)}, f32[32,256,128]{2,1,0:T(8,128)S(1)}, u32[]{:S(2)}) %copy-start) | copy-done | bytes 4194328
  44.4 1.7 %collective-permute-start.4 = (f32[288,128]{1,0:T(8,128)S(1)}, f32[288,128]{1,0:T(8,128)S(1)}, u32[]{:S(2)}, u32[]{:S(2)}) collective-permute-start(f32[288,128]{1,0:T(8,128)S(1)} %slice_select_fusion), channel_id=1, source_target_pairs={{0,32},{32,0},{64,96},{96,64},{128,160},{160,128},{192,224},{224,1... | collective-permute-start | bytes 442376 | tf_op jit(solution)/shard_map/ppermute | solution.py:218
  47.3 3.2 %collective-permute-done.5 = f32[144,128]{1,0:T(8,128)S(1)} collective-permute-done((f32[144,128]{1,0:T(8,128)S(1)}, f32[144,128]{1,0:T(8,128)S(1)}, u32[]{:S(2)}, u32[]{:S(2)}) %collective-permute-start.5) | collective-permute-done | bytes 73760 | tf_op jit(solution)/shard_map/ppermute | solution.py:218
  51.3 3.3 %collective-permute-done.6 = f32[72,128]{1,0:T(8,128)S(1)} collective-permute-done((f32[72,128]{1,0:T(8,128)S(1)}, f32[72,128]{1,0:T(8,128)S(1)}, u32[]{:S(2)}, u32[]{:S(2)}) %collective-permute-start.6) | collective-permute-done | bytes 36896 | tf_op jit(solution)/shard_map/ppermute | solution.py:218
  54.6 2.1 %collective-permute-start.7 = (f32[72,128]{1,0:T(8,128)S(1)}, f32[72,128]{1,0:T(8,128)S(1)}, u32[]{:S(2)}, u32[]{:S(2)}) collective-permute-start(f32[72,128]{1,0:T(8,128)S(1)} %select_add_fusion.2), channel_id=1, source_target_pairs={{0,1},{1,0},{2,3},{3,2},{4,5},{5,4},{6,7},{7,6},{8,9},{9,8},{10,11... | collective-permute-start | bytes 110600 | tf_op jit(solution)/shard_map/ppermute | solution.py:218
  56.8 1.3 %collective-permute-done.7 = f32[72,128]{1,0:T(8,128)S(1)} collective-permute-done((f32[72,128]{1,0:T(8,128)S(1)}, f32[72,128]{1,0:T(8,128)S(1)}, u32[]{:S(2)}, u32[]{:S(2)}) %collective-permute-start.7) | collective-permute-done | bytes 36896 | tf_op jit(solution)/shard_map/ppermute | solution.py:218
  58.1 2.7 %collective-permute-start.8 = (f32[72,128]{1,0:T(8,128)S(1)}, f32[72,128]{1,0:T(8,128)S(1)}, u32[]{:S(2)}, u32[]{:S(2)}) collective-permute-start(f32[72,128]{1,0:T(8,128)S(1)} %add.35), channel_id=1, source_target_pairs={{0,3},{1,2},{2,1},{3,0},{4,7},{5,6},{6,5},{7,4},{8,11},{9,10},{10,... | collective-permute-start | bytes 110600 | tf_op jit(solution)/shard_map/ppermute | solution.py:218
  62.2 4.6 %collective-permute-start.9 = (f32[72,128]{1,0:T(8,128)S(1)}, f32[72,128]{1,0:T(8,128)S(1)}, u32[]{:S(2)}, u32[]{:S(2)}) collective-permute-start(f32[72,128]{1,0:T(8,128)S(1)} %add.36), channel_id=1, source_target_pairs={{0,4},{1,5},{2,6},{3,7},{4,0},{5,1},{6,2},{7,3},{8,12},{9,13},{10,... | collective-permute-start | bytes 110600 | tf_op jit(solution)/shard_map/ppermute | solution.py:218
  68.2 3.0 %collective-permute-start.10 = (f32[72,128]{1,0:T(8,128)S(1)}, f32[72,128]{1,0:T(8,128)S(1)}, u32[]{:S(2)}, u32[]{:S(2)}) collective-permute-start(f32[72,128]{1,0:T(8,128)S(1)} %add.37), channel_id=1, source_target_pairs={{0,8},{1,9},{2,10},{3,11},{4,12},{5,13},{6,14},{7,15},{8,0},{9,1},... | collective-permute-start | bytes 110600 | tf_op jit(solution)/shard_map/ppermute | solution.py:218
  72.5 6.1 %collective-permute-start.11 = (f32[72,128]{1,0:T(8,128)S(1)}, f32[72,128]{1,0:T(8,128)S(1)}, u32[]{:S(2)}, u32[]{:S(2)}) collective-permute-start(f32[72,128]{1,0:T(8,128)S(1)} %add.38), channel_id=1, source_target_pairs={{0,24},{1,25},{2,26},{3,27},{4,28},{5,29},{6,30},{7,31},{8,16},{9,... | collective-permute-start | bytes 110600 | tf_op jit(solution)/shard_map/ppermute | solution.py:218
  78.6 1.4 %collective-permute-done.11 = f32[72,128]{1,0:T(8,128)S(1)} collective-permute-done((f32[72,128]{1,0:T(8,128)S(1)}, f32[72,128]{1,0:T(8,128)S(1)}, u32[]{:S(2)}, u32[]{:S(2)}) %collective-permute-start.11) | collective-permute-done | bytes 36896 | tf_op jit(solution)/shard_map/ppermute | solution.py:218
  80.0 2.1 %collective-permute-start.12 = (f32[72,128]{1,0:T(8,128)S(1)}, f32[72,128]{1,0:T(8,128)S(1)}, u32[]{:S(2)}, u32[]{:S(2)}) collective-permute-start(f32[72,128]{1,0:T(8,128)S(1)} %add.39), channel_id=1, source_target_pairs={{0,192},{32,224},{64,128},{96,160},{128,64},{160,96},{192,0},{224,... | collective-permute-start | bytes 110600 | tf_op jit(solution)/shard_map/ppermute | solution.py:218
  82.1 1.9 %collective-permute-done.12 = f32[72,128]{1,0:T(8,128)S(1)} collective-permute-done((f32[72,128]{1,0:T(8,128)S(1)}, f32[72,128]{1,0:T(8,128)S(1)}, u32[]{:S(2)}, u32[]{:S(2)}) %collective-permute-start.12) | collective-permute-done | bytes 36896 | tf_op jit(solution)/shard_map/ppermute | solution.py:218
  84.1 3.5 %collective-permute-done.13 = f32[144,128]{1,0:T(8,128)S(1)} collective-permute-done((f32[144,128]{1,0:T(8,128)S(1)}, f32[144,128]{1,0:T(8,128)S(1)}, u32[]{:S(2)}, u32[]{:S(2)}) %collective-permute-start.13) | collective-permute-done | bytes 73760 | tf_op jit(solution)/shard_map/ppermute | solution.py:218
  87.7 10.4 %collective-permute-start.14 = (f32[288,128]{1,0:T(8,128)S(1)}, f32[288,128]{1,0:T(8,128)S(1)}, u32[]{:S(2)}, u32[]{:S(2)}) collective-permute-start(f32[288,128]{1,0:T(8,128)S(1)} %pad_maximum_fusion.1), channel_id=1, source_target_pairs={{0,32},{32,0},{64,96},{96,64},{128,160},{160,128},{192,224},{224,1... | collective-permute-start | bytes 442376 | tf_op jit(solution)/shard_map/ppermute | solution.py:218
  99.2 11.7 %factors.1 = (f32[256,256]{1,0:T(8,128)S(1)}, f32[8,256]{1,0:T(8,128)S(1)}, f32[256,256]{1,0:T(8,128)}) custom-call(f32[576,128]{1,0:T(8,128)S(1)} %pad_maximum_fusion.pack_ref), custom_call_target="tpu_custom_call" | custom-call | tf_op jit(solution)/shard_map/factors/pallas_call | solution.py:351
  110.9 2.2 %copy-done.1 = f32[32,256,128]{2,1,0:T(8,128)S(1)} copy-done((f32[32,256,128]{2,1,0:T(8,128)S(1)}, f32[32,256,128]{2,1,0:T(8,128)}, u32[]{:S(2)}) %copy-start.1) | copy-done | bytes 4194328
  113.1 7.2 %apply.1 = (f32[256,32,128]{2,1,0:T(8,128)}, f32[32,128]{1,0:T(8,128)}) custom-call(f32[32,256,128]{2,1,0:T(8,128)S(1)} %copy-done.1, f32[256,256]{1,0:T(8,128)S(1)} %get-tuple-element.23.linv_ref, f32[8,256]{1,0:T(8,128)S(1)} %get-tuple-element.24.coef_ref, f32[32,128]{1,0:T(8,128)S(1)} %get-tuple-element.25.fore_ref), custom_call_target="tpu_custom_call" | custom-call | tf_op jit(solution)/shard_map/apply/pallas_call | solution.py:379
  (51 shorter events, 10.4 us)
Async XLA Ops:
  1.4 20.2 %copy-start.9 = (f32[1,1,64]{2,1,0:T(1,128)S(1)}, f32[1,1,64]{2,1,0:T(1,128)}, u32[]{:S(2)}) copy-start(f32[1,1,64]{2,1,0:T(1,128)} %param.14) | copy-start | bytes 772
  1.4 20.2 %copy-start.10 = (f32[1,1,64]{2,1,0:T(1,128)S(1)}, f32[1,1,64]{2,1,0:T(1,128)}, u32[]{:S(2)}) copy-start(f32[1,1,64]{2,1,0:T(1,128)} %param.15) | copy-start | bytes 772
  1.4 21.3 %copy-start.4 = (f32[32,128]{1,0:T(8,128)S(1)}, f32[32,128]{1,0:T(8,128)}, u32[]{:S(2)}) copy-start(f32[32,128]{1,0:T(8,128)} %mean_ref.3) | copy-start | bytes 49156
  1.4 21.3 %copy-start.5 = (f32[32,128]{1,0:T(8,128)S(1)}, f32[32,128]{1,0:T(8,128)}, u32[]{:S(2)}) copy-start(f32[32,128]{1,0:T(8,128)} %uvel_ref.1) | copy-start | bytes 49156
  1.4 21.4 %copy-start.6 = (f32[32,128]{1,0:T(8,128)S(1)}, f32[32,128]{1,0:T(8,128)}, u32[]{:S(2)}) copy-start(f32[32,128]{1,0:T(8,128)} %vvel_ref.1) | copy-start | bytes 49156
  1.4 21.4 %copy-start.7 = (s32[32,128]{1,0:T(8,128)S(1)}, s32[32,128]{1,0:T(8,128)}, u32[]{:S(2)}) copy-start(s32[32,128]{1,0:T(8,128)} %mask_ref.1) | copy-start | bytes 49156
  1.4 21.4 %copy-start.8 = (s32[1,1,64]{2,1,0:T(1,128)S(1)}, s32[1,1,64]{2,1,0:T(1,128)}, u32[]{:S(2)}) copy-start(s32[1,1,64]{2,1,0:T(1,128)} %index_ref.1) | copy-start | bytes 772
  7.1 2.0 %copy-start.2 = (f32[32,256,128]{2,1,0:T(8,128)}, f32[32,256,128]{2,1,0:T(8,128)S(1)}, u32[]{:S(2)}) copy-start(f32[32,256,128]{2,1,0:T(8,128)S(1)} %get-tuple-element.16.slab_ref) | copy-start | bytes 12582916
  9.2 13.5 %collective-permute-start = (f32[264,128]{1,0:T(8,128)S(1)}, f32[264,128]{1,0:T(8,128)S(1)}, u32[]{:S(2)}, u32[]{:S(2)}) collective-permute-start(f32[264,128]{1,0:T(8,128)S(1)} %get-tuple-element.17), channel_id=1, source_target_pairs={{32,0},{64,32},{96,64},{128,96},{160,128},{192,160},{224,192},{33,... | collective-permute-start | bytes 405512 | tf_op jit(solution)/shard_map/ppermute | solution.py:406
  14.3 8.4 %collective-permute-start.1 = (f32[264,128]{1,0:T(8,128)S(1)}, f32[264,128]{1,0:T(8,128)S(1)}, u32[]{:S(2)}, u32[]{:S(2)}) collective-permute-start(f32[264,128]{1,0:T(8,128)S(1)} %get-tuple-element.18), channel_id=1, source_target_pairs={{0,32},{32,64},{64,96},{96,128},{128,160},{160,192},{192,224},{1,3... | collective-permute-start | bytes 405512 | tf_op jit(solution)/shard_map/ppermute | solution.py:407
  16.2 5.4 %collective-permute-start.2 = (f32[96,128]{1,0:T(8,128)S(1)}, f32[96,128]{1,0:T(8,128)S(1)}, u32[]{:S(2)}, u32[]{:S(2)}) collective-permute-start(f32[96,128]{1,0:T(8,128)S(1)} %get-tuple-element.19), channel_id=1, source_target_pairs={{1,0},{2,1},{3,2},{4,3},{5,4},{6,5},{7,6},{8,7},{9,8},{10,9},{11,1... | collective-permute-start | bytes 147464 | tf_op jit(solution)/shard_map/ppermute | solution.py:408
  17.5 5.2 %collective-permute-start.3 = (f32[96,128]{1,0:T(8,128)S(1)}, f32[96,128]{1,0:T(8,128)S(1)}, u32[]{:S(2)}, u32[]{:S(2)}) collective-permute-start(f32[96,128]{1,0:T(8,128)S(1)} %get-tuple-element.20), channel_id=1, source_target_pairs={{0,1},{1,2},{2,3},{3,4},{4,5},{5,6},{6,7},{7,8},{8,9},{9,10},{10,1... | collective-permute-start | bytes 147464 | tf_op jit(solution)/shard_map/ppermute | solution.py:409
  44.4 2.7 %collective-permute-start.4 = (f32[288,128]{1,0:T(8,128)S(1)}, f32[288,128]{1,0:T(8,128)S(1)}, u32[]{:S(2)}, u32[]{:S(2)}) collective-permute-start(f32[288,128]{1,0:T(8,128)S(1)} %slice_select_fusion), channel_id=1, source_target_pairs={{0,32},{32,0},{64,96},{96,64},{128,160},{160,128},{192,224},{224,1... | collective-permute-start | bytes 442376 | tf_op jit(solution)/shard_map/ppermute | solution.py:218
  47.2 3.3 %collective-permute-start.5 = (f32[144,128]{1,0:T(8,128)S(1)}, f32[144,128]{1,0:T(8,128)S(1)}, u32[]{:S(2)}, u32[]{:S(2)}) collective-permute-start(f32[144,128]{1,0:T(8,128)S(1)} %slice_select_fusion.1), channel_id=1, source_target_pairs={{0,64},{32,96},{64,0},{96,32},{128,192},{160,224},{192,128},{224,1... | collective-permute-start | bytes 221192 | tf_op jit(solution)/shard_map/ppermute | solution.py:218
  50.5 4.1 %collective-permute-start.6 = (f32[72,128]{1,0:T(8,128)S(1)}, f32[72,128]{1,0:T(8,128)S(1)}, u32[]{:S(2)}, u32[]{:S(2)}) collective-permute-start(f32[72,128]{1,0:T(8,128)S(1)} %slice_select_fusion.2), channel_id=1, source_target_pairs={{0,192},{32,224},{64,128},{96,160},{128,64},{160,96},{192,0},{224,... | collective-permute-start | bytes 110600 | tf_op jit(solution)/shard_map/ppermute | solution.py:218
  54.6 3.5 %collective-permute-start.7 = (f32[72,128]{1,0:T(8,128)S(1)}, f32[72,128]{1,0:T(8,128)S(1)}, u32[]{:S(2)}, u32[]{:S(2)}) collective-permute-start(f32[72,128]{1,0:T(8,128)S(1)} %select_add_fusion.2), channel_id=1, source_target_pairs={{0,1},{1,0},{2,3},{3,2},{4,5},{5,4},{6,7},{7,6},{8,9},{9,8},{10,11... | collective-permute-start | bytes 110600 | tf_op jit(solution)/shard_map/ppermute | solution.py:218
  58.1 4.1 %collective-permute-start.8 = (f32[72,128]{1,0:T(8,128)S(1)}, f32[72,128]{1,0:T(8,128)S(1)}, u32[]{:S(2)}, u32[]{:S(2)}) collective-permute-start(f32[72,128]{1,0:T(8,128)S(1)} %add.35), channel_id=1, source_target_pairs={{0,3},{1,2},{2,1},{3,0},{4,7},{5,6},{6,5},{7,4},{8,11},{9,10},{10,... | collective-permute-start | bytes 110600 | tf_op jit(solution)/shard_map/ppermute | solution.py:218
  62.2 5.9 %collective-permute-start.9 = (f32[72,128]{1,0:T(8,128)S(1)}, f32[72,128]{1,0:T(8,128)S(1)}, u32[]{:S(2)}, u32[]{:S(2)}) collective-permute-start(f32[72,128]{1,0:T(8,128)S(1)} %add.36), channel_id=1, source_target_pairs={{0,4},{1,5},{2,6},{3,7},{4,0},{5,1},{6,2},{7,3},{8,12},{9,13},{10,... | collective-permute-start | bytes 110600 | tf_op jit(solution)/shard_map/ppermute | solution.py:218
  68.2 4.3 %collective-permute-start.10 = (f32[72,128]{1,0:T(8,128)S(1)}, f32[72,128]{1,0:T(8,128)S(1)}, u32[]{:S(2)}, u32[]{:S(2)}) collective-permute-start(f32[72,128]{1,0:T(8,128)S(1)} %add.37), channel_id=1, source_target_pairs={{0,8},{1,9},{2,10},{3,11},{4,12},{5,13},{6,14},{7,15},{8,0},{9,1},... | collective-permute-start | bytes 110600 | tf_op jit(solution)/shard_map/ppermute | solution.py:218
  72.5 7.5 %collective-permute-start.11 = (f32[72,128]{1,0:T(8,128)S(1)}, f32[72,128]{1,0:T(8,128)S(1)}, u32[]{:S(2)}, u32[]{:S(2)}) collective-permute-start(f32[72,128]{1,0:T(8,128)S(1)} %add.38), channel_id=1, source_target_pairs={{0,24},{1,25},{2,26},{3,27},{4,28},{5,29},{6,30},{7,31},{8,16},{9,... | collective-permute-start | bytes 110600 | tf_op jit(solution)/shard_map/ppermute | solution.py:218
  80.0 4.0 %collective-permute-start.12 = (f32[72,128]{1,0:T(8,128)S(1)}, f32[72,128]{1,0:T(8,128)S(1)}, u32[]{:S(2)}, u32[]{:S(2)}) collective-permute-start(f32[72,128]{1,0:T(8,128)S(1)} %add.39), channel_id=1, source_target_pairs={{0,192},{32,224},{64,128},{96,160},{128,64},{160,96},{192,0},{224,... | collective-permute-start | bytes 110600 | tf_op jit(solution)/shard_map/ppermute | solution.py:218
  84.0 3.6 %collective-permute-start.13 = (f32[144,128]{1,0:T(8,128)S(1)}, f32[144,128]{1,0:T(8,128)S(1)}, u32[]{:S(2)}, u32[]{:S(2)}) collective-permute-start(f32[144,128]{1,0:T(8,128)S(1)} %pad_maximum_fusion.2), channel_id=1, source_target_pairs={{0,64},{32,96},{64,0},{96,32},{128,192},{160,224},{192,128},{224,1... | collective-permute-start | bytes 221192 | tf_op jit(solution)/shard_map/ppermute | solution.py:218
  87.7 11.5 %collective-permute-start.14 = (f32[288,128]{1,0:T(8,128)S(1)}, f32[288,128]{1,0:T(8,128)S(1)}, u32[]{:S(2)}, u32[]{:S(2)}) collective-permute-start(f32[288,128]{1,0:T(8,128)S(1)} %pad_maximum_fusion.1), channel_id=1, source_target_pairs={{0,32},{32,0},{64,96},{96,64},{128,160},{160,128},{192,224},{224,1... | collective-permute-start | bytes 442376 | tf_op jit(solution)/shard_map/ppermute | solution.py:218
  110.9 2.2 %copy-start.1 = (f32[32,256,128]{2,1,0:T(8,128)S(1)}, f32[32,256,128]{2,1,0:T(8,128)}, u32[]{:S(2)}) copy-start(f32[32,256,128]{2,1,0:T(8,128)} %copy-done) | copy-start | bytes 12582916
  (2 other events, 2.7 us)

commit v3 on v2

v3 whole, which is shorter than its diff:
```python
import functools

import jax
import jax.numpy as jnp
from jax import lax
from jax.experimental import pallas as pl
from jax.experimental.pallas import tpu as pltpu
from jax.sharding import Mesh
from jax.sharding import PartitionSpec as P

HIGH = lax.Precision.HIGHEST
PANEL = 16
LANES = 128
PACK = 576
VMEM = pl.BlockSpec(memory_space=pltpu.VMEM)
HBM = pl.BlockSpec(memory_space=pltpu.HBM)


def room(mebibytes):
    return pltpu.CompilerParams(vmem_limit_bytes=mebibytes * 2**20)


def high_dot(a, b, dims):
    return lax.dot_general(
        a, b, (dims, ((), ())), precision=HIGH, preferred_element_type=jnp.float32
    )


def lanes_of(shape):
    return lax.broadcasted_iota(jnp.int32, shape, len(shape) - 1)


def by_latitude(block, first):
    count = block.shape[0]
    turned = [jnp.swapaxes(block[r : r + 8, first : first + 8, :], 0, 1) for r in range(0, count, 8)]
    return [jnp.concatenate([part[e] for part in turned], axis=0) for e in range(8)]


def reads_of(source, target, sems):
    rows = target.shape[1]
    copies = [
        pltpu.make_async_copy(source.at[pl.ds(i * rows, rows)], target.at[i], sems.at[i])
        for i in range(target.shape[0])
    ]
    for copy in copies:
        copy.start()
    return copies


def edges_kernel(modes_ref, mean_ref, low_ref, high_ref, west_ref, east_ref, block, in_sem, mean_sem):
    chunks, rows, lats, lons = block.shape
    groups = lons // lats
    total = chunks * rows
    packed = total // groups
    reads = reads_of(modes_ref, block, in_sem)
    means = [
        pltpu.make_async_copy(mean_ref, side.at[pl.ds(packed, lats)], mean_sem.at[i])
        for i, side in enumerate((west_ref, east_ref))
    ]
    for copy in means:
        copy.start()
    lane = lanes_of((rows, lons))
    for i in range(chunks):
        base = i * rows // packed * lats
        here = slice(i * rows % packed, i * rows % packed + rows)
        span = slice(i * rows, (i + 1) * rows)
        reads[i].wait()
        west = jnp.zeros((rows, lons), jnp.float32) if base == 0 else west_ref[here]
        east = jnp.zeros((rows, lons), jnp.float32) if base == 0 else east_ref[here]
        for first in range(0, lats, 8):
            for e, line in enumerate(by_latitude(block.at[i], first)):
                lat = first + e
                moved = pltpu.roll(line, (base + lat + 1) % lons, 1)
                west = jnp.where(lane == (base + lat + 1) % lons, moved, west)
                east = jnp.where(lane == base + lat, moved, east)
                if lat == 0:
                    low_ref[span] = line
                if lat == lats - 1:
                    high_ref[span] = line
        west_ref[here] = west
        east_ref[here] = east
    for copy in means:
        copy.wait()
    low_ref[total : total + 8] = jnp.broadcast_to(west_ref[packed : packed + 1], (8, lons))
    high_ref[total : total + 8] = jnp.broadcast_to(west_ref[packed + lats - 1 : packed + lats], (8, lons))


def edges_of(modes, mean_state):
    count, lats, lons = modes.shape
    packed = count * lats // lons
    chunks = 8
    sides = [(count + 8, lons), (count + 8, lons), (packed + lats, lons), (packed + lats, lons)]
    return pl.pallas_call(
        edges_kernel,
        in_specs=[HBM] * 2,
        out_specs=[VMEM] * 4,
        out_shape=[jax.ShapeDtypeStruct(s, jnp.float32) for s in sides],
        scratch_shapes=[
            pltpu.VMEM((chunks, count // chunks, lats, lons), jnp.float32),
            pltpu.SemaphoreType.DMA((chunks,)),
            pltpu.SemaphoreType.DMA((2,)),
        ],
        compiler_params=room(61),
        name="edges",
    )(modes, mean_state)


def split(value):
    top = value.astype(jnp.bfloat16)
    return top, (value - top.astype(jnp.float32)).astype(jnp.bfloat16)


def pair_rows(a, b):
    return lax.dot_general(a, b, (((1,), (1,)), ((), ())), preferred_element_type=jnp.float32)


def sums_kernel(
    modes_ref, mean_ref, north_ref, south_ref, east_ref, west_ref, uvel_ref, vvel_ref, mask_ref,
    index_ref, value_ref, weight_ref, adv_hbm, fore_ref, pack_ref, slab_ref, adv_ref, coef, parts, seen, out_sem,
):
    lats, count, lons = slab_ref.shape
    chunks = out_sem.shape[0]
    deep = lats // chunks
    writes = []
    for i in range(chunks):
        span = pl.ds(i * deep, deep)
        writes.append(pltpu.make_async_copy(adv_ref.at[span], adv_hbm.at[span], out_sem.at[i]))
    groups = lons // lats
    rows = count // groups
    for r in range(0, count, rows):
        for lat in range(0, lats, 8):
            for e, line in enumerate(by_latitude(modes_ref.at[r : r + rows], lat)):
                slab_ref[lat + e, r : r + rows, :] = line
    sea = mask_ref[...].astype(jnp.float32)
    half_u, half_v = 0.5 * uvel_ref[...], 0.5 * vvel_ref[...]
    coef[0] = sea * 0.2
    coef[1] = sea * (0.2 - half_u)
    coef[2] = sea * (0.2 + half_u)
    coef[3] = sea * (0.2 - half_v)
    coef[4] = sea * (0.2 + half_v)
    first = lanes_of((lats, lons)) == 0
    last = lanes_of((lats, lons)) == lons - 1
    mean = mean_ref[...]
    eastern = jnp.where(last, east_ref[rows : rows + lats, 0:1], pltpu.roll(mean, lons - 1, 1))
    western = jnp.where(first, west_ref[rows : rows + lats, lons - 1 : lons], pltpu.roll(mean, 1, 1))
    northern = jnp.concatenate([mean[1:], north_ref[count : count + 1]], axis=0)
    southern = jnp.concatenate([south_ref[count : count + 1], mean[:-1]], axis=0)
    fore = coef[0] * mean + coef[1] * eastern + coef[2] * western
    fore_ref[...] = fore + coef[3] * northern + coef[4] * southern

    first = lanes_of((rows, lons)) == 0
    last = lanes_of((rows, lons)) == lons - 1

    def advance(lat, northern, southern):
        factors = [coef[i, pl.ds(lat, 1), :] for i in range(5)]
        out = []
        for g in range(groups):
            span = slice(g * rows, (g + 1) * rows)
            centre = slab_ref[lat, span, :]
            east_edge = pltpu.roll(east_ref[0:rows], (lons - 2 - g * lats - lat) % lons, 1)
            west_edge = pltpu.roll(west_ref[0:rows], (-g * lats - lat) % lons, 1)
            eastern = jnp.where(last, east_edge, pltpu.roll(centre, lons - 1, 1))
            western = jnp.where(first, west_edge, pltpu.roll(centre, 1, 1))
            moved = factors[0] * centre + factors[1] * eastern + factors[2] * western
            moved = moved + factors[3] * northern[span, :] + factors[4] * southern[span, :]
            adv_ref[lat, span, :] = moved
            out.append(moved)
        return jnp.concatenate(out, axis=0)

    observed = index_ref.shape[-1]
    point = index_ref[...]
    square = (observed, observed)
    eye = lax.broadcasted_iota(jnp.int32, square, 0) == lanes_of(square)
    point_col = jnp.sum(jnp.where(eye, point.astype(jnp.float32), 0.0), axis=1, keepdims=True)
    away = point_col.astype(jnp.int32) - lanes_of((observed, 2 * lons))

    parts[...] = jnp.zeros_like(parts)
    seen[...] = jnp.zeros_like(seen)
    for lat in range(0, lats, 2):
        rows_of = lambda i: south_ref if i < 0 else north_ref if i == lats else slab_ref.at[i]
        pair = [advance(i, rows_of(i + 1), rows_of(i - 1)) for i in (lat, lat + 1)]
        top, low = split(jnp.concatenate(pair, axis=1))
        parts[0] += pair_rows(top, top) + pair_rows(low, low)
        parts[1] += pair_rows(top, low)
        pick = jnp.where(away == lat * lons, 1.0, 0.0).astype(jnp.bfloat16)
        seen[...] += pair_rows(top, pick) + pair_rows(low, pick)
        if (lat + 2) % deep == 0:
            writes[lat // deep].start()

    lon_pick = jnp.where(lax.rem(point_col.astype(jnp.int32), lons) == lanes_of((observed, lons)), 1.0, 0.0)
    fore_at = high_dot(fore_ref[...], lon_pick, ((1,), (1,)))
    lat_of = lax.broadcasted_iota(jnp.int32, (lats, observed), 0)
    fore_at = jnp.sum(jnp.where(lat_of == point // lons, fore_at, 0.0), axis=0, keepdims=True)
    weights = weight_ref[...]
    diff = value_ref[...] - fore_at
    found = seen[...]
    obs_c = high_dot(found * weights, found, ((1,), (1,)))
    obs_b = high_dot(jnp.broadcast_to(weights * diff, (8, observed)), found, ((1,), (1,)))
    cross = parts[1]
    gram = parts[0] + (cross + cross.T)
    row = lax.broadcasted_iota(jnp.int32, (count, count), 0)
    col = lax.broadcasted_iota(jnp.int32, (count, count), 1)
    both = jnp.where(row >= col, gram, obs_c)
    diag_c = jnp.sum(jnp.where(row == col, obs_c, 0.0), axis=0, keepdims=True)
    pack_ref[0:count] = both[:, 0:lons]
    pack_ref[count : 2 * count] = both[:, lons:]
    pack_ref[2 * count :] = jnp.zeros((PACK - 2 * count, lons), jnp.float32)
    for i, line in enumerate((diag_c, obs_b[0:1])):
        pack_ref[2 * count + 2 * i : 2 * count + 2 * i + 1] = line[:, 0:lons]
        pack_ref[2 * count + 2 * i + 1 : 2 * count + 2 * i + 2] = line[:, lons:]
    for copy in writes:
        copy.wait()


def sums_of(modes, mean_state, sides, east_vel, north_vel, sea_mask, obs_index, obs_value, obs_weight):
    count, lats, lons = modes.shape
    line = lambda x: x.reshape(1, -1)
    return pl.pallas_call(
        sums_kernel,
        in_specs=[VMEM] * 12,
        out_specs=[HBM] + [VMEM] * 2,
        out_shape=[
            jax.ShapeDtypeStruct((lats, count, lons), jnp.float32),
            jax.ShapeDtypeStruct((lats, lons), jnp.float32),
            jax.ShapeDtypeStruct((PACK, lons), jnp.float32),
        ],
        scratch_shapes=[
            pltpu.VMEM((lats, count, lons), jnp.float32),
            pltpu.VMEM((lats, count, lons), jnp.float32),
            pltpu.VMEM((5, lats, lons), jnp.float32),
            pltpu.VMEM((2, count, count), jnp.float32),
            pltpu.VMEM((count, obs_index.size), jnp.float32),
            pltpu.SemaphoreType.DMA((8,)),
        ],
        compiler_params=room(50),
        name="sums",
    )(modes, mean_state, *sides, east_vel, north_vel, sea_mask, line(obs_index), line(obs_value), line(obs_weight))


def swap(value, axis, first):
    lower = range(first, lax.axis_size(axis) - 1, 2)
    pairs = [(i, i + 1) for i in lower] + [(i + 1, i) for i in lower]
    return lax.ppermute(value, axis, pairs)


def scatter_sum(value, axes):
    count = lax.axis_size(axes)
    return lax.all_to_all(value.reshape(count, -1, LANES), axes, 0, 0).sum(0)


def gather(value, axes):
    return lax.all_to_all(jnp.broadcast_to(value[None], (lax.axis_size(axes),) + value.shape), axes, 0, 0)


def sum_everywhere(value):
    half = value.shape[0] // 2
    low, high = value[:half], value[half:]
    upper = lax.axis_index("core") == 1
    value = jnp.where(upper, high, low) + swap(jnp.where(upper, low, high), "core", 0)
    value = scatter_sum(value, ("x", "y"))
    value = gather(value, "z").sum(0)
    value = gather(value, ("x", "y")).reshape(half, LANES)
    other = swap(value, "core", 0)
    return jnp.concatenate([jnp.where(upper, other, value), jnp.where(upper, value, other)])


def factor_panels(work, upper, inverse):
    size = work.shape[1]
    tiles = size // LANES
    lane = lanes_of((PANEL, LANES))
    sub = lax.broadcasted_iota(jnp.int32, (PANEL, LANES), 0)
    lane_row = lanes_of((1, LANES))
    for first in range(0, size, PANEL):
        home, at = first // LANES, first % LANES
        inside = (lane >= at) & (lane < at + PANEL)
        state = []
        for m in range(2):
            rows = [work[m, first : first + PANEL, t * LANES : (t + 1) * LANES] for t in range(tiles)]
            cols = [
                jnp.broadcast_to(rows[home][:, at + k : at + k + 1], (PANEL, LANES))
                for k in range(PANEL)
            ]
            block = jnp.where(inside, rows[home], 0.0)
            rows[home] = jnp.where(inside, jnp.where(lane == sub + at, 1.0, 0.0), rows[home])
            state.append((rows + [block], cols))
        for j in range(0, PANEL, 2):
            pair = (sub == j) | (sub == j + 1)
            for m in range(2):
                rows, cols = state[m]
                c0, c1 = cols[j], cols[j + 1]
                a, b, d = c0[j : j + 1], c1[j : j + 1], c1[j + 1 : j + 2]
                rdet = 1.0 / (a * d - b * b)
                i00, i01, i11 = d * rdet, -b * rdet, a * rdet
                m0 = c0 * i00 + c1 * i01
                m1 = c0 * i01 + c1 * i11
                m0 = jnp.where(sub == j, -i00, jnp.where(sub == j + 1, -i01, m0))
                m1 = jnp.where(sub == j, -i01, jnp.where(sub == j + 1, -i11, m1))
                for k in range(j + 2, PANEL):
                    ck = cols[k]
                    cols[k] = jnp.where(pair, 0.0, ck) - m0 * ck[j : j + 1] - m1 * ck[j + 1 : j + 2]
                ra = lax.rsqrt(a)
                ra = ra * (1.5 - 0.5 * a * ra * ra)
                ratio = b * ra * ra
                rest = d - ratio * b
                rb = lax.rsqrt(rest)
                rb = rb * (1.5 - 0.5 * rest * rb * rb)
                for t in range(tiles + 1):
                    r0, r1 = rows[t][j : j + 1], rows[t][j + 1 : j + 2]
                    done = (r0 * ra, (r1 - ratio * r0) * rb)
                    rows[t] = jnp.where(pair, 0.0, rows[t]) - m0 * r0 - m1 * r1
                    if t == tiles:
                        extra = done
                    elif t == home:
                        mine = done
                    else:
                        target, other = (inverse, upper) if t < home else (upper, inverse)
                        span = slice(t * LANES, (t + 1) * LANES)
                        target[m, first + j : first + j + 1, span] = done[0]
                        target[m, first + j + 1 : first + j + 2, span] = done[1]
                        other[m, first + j : first + j + 2, span] = jnp.zeros((2, LANES), jnp.float32)
                span = slice(home * LANES, (home + 1) * LANES)
                for e in range(2):
                    row = slice(first + j + e, first + j + e + 1)
                    left = lane_row < at + PANEL
                    inverse[m, row, span] = jnp.where(left, mine[e], 0.0)
                    corner = jnp.where(lane_row >= at + j + e, extra[e], 0.0)
                    upper[m, row, span] = jnp.where(left, corner, mine[e])
        for m in range(2):
            panel = jnp.concatenate(state[m][0][:tiles], axis=1)
            blocks = [panel]
            if at:
                blocks.insert(0, jnp.zeros((at, size), jnp.float32))
            if at + PANEL < LANES:
                blocks.append(jnp.zeros((LANES - at - PANEL, size), jnp.float32))
            panel = jnp.concatenate(blocks, axis=0)
            for start, stop in ((first + PANEL, first + 2 * PANEL), (first + 2 * PANEL, size)):
                if start >= min(stop, size):
                    continue
                left = work[m, start:stop, home * LANES : (home + 1) * LANES]
                change = high_dot(left, panel, ((1,), (0,)))
                place = lanes_of(left.shape)
                for t in range(tiles):
                    span = slice(t * LANES, (t + 1) * LANES)
                    if t == home:
                        old = jnp.where((place >= at) & (place < at + PANEL), 0.0, left)
                    else:
                        old = work[m, start:stop, span]
                    work[m, start:stop, span] = old - change[:, span]


def finish_kernel(
    scale, pack_ref, adv_hbm, fore_ref, mean_ref, basis_hbm, root_hbm,
    work, upper, inverse, root, adv, basis, in_sem, out_sem, root_sem,
):
    lats, size, lons = adv.shape
    steps = in_sem.shape[0]
    deep = lats // steps
    reads, writes = [], []
    for i in range(steps):
        span = pl.ds(i * deep, deep)
        reads.append(pltpu.make_async_copy(adv_hbm.at[span], adv.at[span], in_sem.at[i]))
        writes.append(pltpu.make_async_copy(basis.at[i], basis_hbm.at[:, span, :], out_sem.at[i]))
        reads[i].start()
    row = lax.broadcasted_iota(jnp.int32, (size, size), 0)
    col = lax.broadcasted_iota(jnp.int32, (size, size), 1)
    eye = row == col
    both = jnp.concatenate([pack_ref[0:size], pack_ref[size : 2 * size]], axis=1)
    turned = both.T
    line = lambda i: jnp.concatenate(
        [pack_ref[2 * size + i : 2 * size + i + 1], pack_ref[2 * size + i + 1 : 2 * size + i + 2]], axis=1
    )
    gram = jnp.where(row >= col, both, turned)
    obs_c = jnp.where(row < col, both, jnp.where(eye, line(0), turned))
    only = jnp.where(eye, both, 0.0)
    q_row = lax.rsqrt(jnp.sum(only, axis=0, keepdims=True))
    work[0] = gram * q_row * lax.rsqrt(jnp.sum(only, axis=1, keepdims=True))
    work[1] = jnp.where(eye, 1.0, 0.0) + obs_c / (size - 1.0)
    factor_panels(work, upper, inverse)
    finv = inverse[1]
    half = high_dot(jnp.broadcast_to(line(2), (8, size)), finv, ((1,), (1,)))
    coef = high_dot(half, finv, ((1,), (0,))) / (size - 1.0)
    left = jnp.concatenate([inverse[0] * (q_row * scale), coef], axis=0)
    for i in range(steps):
        reads[i].wait()
        wide = jnp.concatenate([adv[i * deep + e] for e in range(deep)], axis=1)
        out = high_dot(left, wide, ((1,), (0,)))
        parts = [out[:, e * lons : (e + 1) * lons] for e in range(deep)]
        for r in range(0, size, 8):
            basis[i, r : r + 8] = jnp.swapaxes(jnp.stack([part[r : r + 8] for part in parts]), 0, 1)
        writes[i].start()
        for e, part in enumerate(parts):
            lat = i * deep + e
            mean_ref[lat : lat + 1] = fore_ref[lat : lat + 1] + part[size : size + 1]
    root[...] = high_dot(upper[0] * ((1.0 / q_row) / scale), finv, ((1,), (1,)))
    writes.append(pltpu.make_async_copy(root, root_hbm, root_sem))
    writes[-1].start()
    for copy in writes:
        copy.wait()


def finish(pack, advanced, fore, scale):
    lats, size, lons = advanced.shape
    steps = 4
    square = (size, size)
    return pl.pallas_call(
        functools.partial(finish_kernel, scale),
        in_specs=[VMEM, HBM, VMEM],
        out_specs=[VMEM, HBM, HBM],
        out_shape=[
            jax.ShapeDtypeStruct((lats, lons), jnp.float32),
            jax.ShapeDtypeStruct((size, lats, lons), jnp.float32),
            jax.ShapeDtypeStruct(square, jnp.float32),
        ],
        scratch_shapes=[pltpu.VMEM((2,) + square, jnp.float32)] * 3
        + [
            pltpu.VMEM(square, jnp.float32),
            pltpu.VMEM((lats, size, lons), jnp.float32),
            pltpu.VMEM((steps, size, lats // steps, lons), jnp.float32),
            pltpu.SemaphoreType.DMA((steps,)),
            pltpu.SemaphoreType.DMA((steps,)),
            pltpu.SemaphoreType.DMA,
        ],
        compiler_params=room(61),
        name="finish",
    )(pack, advanced, fore)


def body(mean_state, modes, east_vel, north_vel, sea_mask, obs_index, obs_value, obs_weight):
    count, lat_rows, lon_cols = modes.shape
    low, high, west, east = edges_of(modes, mean_state)
    band, tile = ("x", "core"), ("z", "y")
    sides = []
    for axis, first, last in ((band, low, high), (tile, west, east)):
        even = lax.axis_index(axis) % 2 == 0
        one = swap(jnp.where(even, last, first), axis, 0)
        two = swap(jnp.where(even, first, last), axis, 1)
        sides += [jnp.where(even, one, two), jnp.where(even, two, one)]
    advanced, fore, pack = sums_of(
        modes, mean_state, sides, east_vel, north_vel, sea_mask, obs_index, obs_value, obs_weight
    )
    pack = sum_everywhere(pack)
    points = lat_rows * lon_cols * lax.axis_size(band) * lax.axis_size(tile)
    mean_analysis, basis, root_factor = finish(pack, advanced, fore, float(points) ** 0.5)
    return (mean_analysis, basis, root_factor)


def solution(mesh):
    mesh = Mesh(mesh.devices.reshape(4, 2, 8, 4), ("x", "core", "z", "y"))
    band, tile = ("x", "core"), ("z", "y")
    grid, blocks = P(band, tile), P(None, band, tile)
    obs = P(band, tile, None)
    return jax.shard_map(
        body,
        mesh=mesh,
        in_specs=(grid, blocks, grid, grid, grid, obs, obs, obs),
        out_specs=(grid, blocks, P()),
        check_vma=False,
    )
```

time: 121 us -> 94.4 us (0.78)
  blocking collectives: 0 us -> 38.6 us
  starting transfers between devices: 46.2 us -> 14.4 us
  waiting for transfers between devices: 21.7 us -> 4.91 us
  Pallas kernels: 44.3 us -> 31.6 us
  local copies, waits for them, and re-layouts: 6.95 us -> 0.67 us
  other arithmetic: 0.2 us -> 2.69 us
    all_to_all x0 -> x3, blocking collectives: none -> 38.6 us  [the longest x2 25 us: gather(): lax.all_to_all(jnp.broadcast_to(value[None], (lax.axis_size(axes),) + val...]
    ppermute x15 -> x6, starting transfers between devices: 46.2 us -> 14.4 us  [swap(): return lax.ppermute(value, axis, pairs)]
    ppermute x15 -> x6, waiting for transfers between devices: 21.7 us -> 4.91 us  [swap(): return lax.ppermute(value, axis, pairs)]
    pallas_call x4 -> x3, Pallas kernels: 44.3 us -> 31.6 us  [the longest x1 19.4 us: finish(): pl.pallas_call(functools.partial(finish_kernel, scale), in_specs=[VMEM, H...]
    unnamed x22 -> x16, local copies, waits for them, and re-layouts: 6.94 us -> 0.62 us
    select_n x0 -> x4, other arithmetic: none -> 1.86 us  [the longest x2 1.82 us: body(): two = swap(jnp.where(even, first, last), axis, 1)]
  transfers between devices with their start and end apart: 15 -> 6, of which waited for: 12 -> 3; matrix products, arithmetic and copies ran while one was open for 0% -> 1% of each run, Pallas kernels for 0% -> 0%
where the time goes in v3:
time: 94.4 us; the launch traced here: 94 us
  blocking collectives  38.6 us (41%)
  Pallas kernels  31.6 us (33%)
  starting transfers between devices  14.4 us (15%)
  waiting for transfers between devices  4.91 us (5%)
  other arithmetic  2.69 us (3%)
  between operations  1.07 us (1%)
    all_to_all x2, blocking collectives, gather(): lax.all_to_all(jnp.broadcast_to(value[None], (lax.axis_size(axes),) + val...  25 us
    pallas_call x1, Pallas kernels, finish(): pl.pallas_call(functools.partial(finish_kernel, scale), in_specs=[VMEM, H...  19.4 us
    ppermute x6, starting transfers between devices, swap(): return lax.ppermute(value, axis, pairs)  14.4 us
    all_to_all x1, blocking collectives, scatter_sum(): return lax.all_to_all(value.reshape(count, -1, LANES), axes, 0, 0).sum(0)  13.6 us
    pallas_call x1, Pallas kernels, sums_of(): pl.pallas_call(sums_kernel, in_specs=[VMEM] * 12, out_specs=[HBM] + [VMEM...  8.58 us
    ppermute x6, waiting for transfers between devices, swap(): return lax.ppermute(value, axis, pairs)  4.91 us
    pallas_call x1, Pallas kernels, edges_of(): pl.pallas_call(edges_kernel, in_specs=[HBM] * 2, out_specs=[VMEM] * 4, ou...  3.7 us
  transfers between devices with their start and end apart: 6, of which 3 were waited for; matrix products, arithmetic and copies ran while one was open for 1% of the time, Pallas kernels for 0%

profile of v3, /device:TPU:1, one launch (start us, length us, event | category | flops | bytes accessed | tf_op | source)
XLA Modules:
  0.0 94.0 jit_solution(17610143749770543504)
XLA Ops:
  0.6 0.0 copy-start
  0.6 0.0 copy-start.7
  0.7 3.7 %edges.1 = (f32[264,128]{1,0:T(8,128)}, f32[264,128]{1,0:T(8,128)}, f32[96,128]{1,0:T(8,128)}, f32[96,128]{1,0:T(8,128)}) custom-call(f32[256,32,128]{2,1,0:T(8,128)} %modes_ref.3, f32[32,128]{1,0:T(8,128)} %mean_ref.3), custom_call_target="tpu_custom_call" | custom-call | tf_op jit(solution)/shard_map/edges/pallas_call | solution.py:93
  4.4 0.8 broadcast_select_fusion.8
  5.3 0.7 collective-permute-start.3
  5.9 4.8 %collective-permute-start.2 = (f32[96,128]{1,0:T(8,128)S(1)}, f32[96,128]{1,0:T(8,128)S(1)}, u32[]{:S(2)}, u32[]{:S(2)}) collective-permute-start(f32[96,128]{1,0:T(8,128)S(1)} %get-tuple-element.26), channel_id=1, source_target_pairs={{0,1},{2,3},{4,5},{6,7},{8,9},{10,11},{12,13},{14,15},{16,17},{18,... | collective-permute-start | bytes 147464 | tf_op jit(solution)/shard_map/ppermute | solution.py:243
  10.7 1.0 %broadcast_select_fusion.4 = (f32[264,128]{1,0:T(8,128)S(1)}, f32[264,128]{1,0:T(8,128)S(1)}) fusion(f32[264,128]{1,0:T(8,128)} %get-tuple-element.11, f32[264,128]{1,0:T(8,128)} %get-tuple-element.10, pred[]{:T(512)S(6)} %eq.13), kind=kLoop, calls=%fused_computation.7 | loop fusion | flops 67584 | bytes 540673 | tf_op jit(solution)/shard_map/jit(_where)/select_n | solution.py:436
  11.7 4.2 %collective-permute-start.1 = (f32[264,128]{1,0:T(8,128)S(1)}, f32[264,128]{1,0:T(8,128)S(1)}, u32[]{:S(2)}, u32[]{:S(2)}) collective-permute-start(f32[264,128]{1,0:T(8,128)S(1)} %get-tuple-element.21), channel_id=1, source_target_pairs={{32,64},{96,128},{160,192},{64,32},{128,96},{192,160},{33,65},{97,... | collective-permute-start | bytes 405512 | tf_op jit(solution)/shard_map/ppermute | solution.py:243
  15.9 0.1 collective-permute-start
  16.0 0.0 collective-permute-done.3
  16.0 0.0 collective-permute-done.2
  16.1 2.5 %collective-permute-done.1 = f32[264,128]{1,0:T(8,128)S(1)} collective-permute-done((f32[264,128]{1,0:T(8,128)S(1)}, f32[264,128]{1,0:T(8,128)S(1)}, u32[]{:S(2)}, u32[]{:S(2)}) %collective-permute-start.1) | collective-permute-done | bytes 135200 | tf_op jit(solution)/shard_map/ppermute | solution.py:243
  18.6 0.0 collective-permute-done
  18.7 8.6 %sums.1 = (f32[32,256,128]{2,1,0:T(8,128)}, f32[32,128]{1,0:T(8,128)S(1)}, f32[576,128]{1,0:T(8,128)S(1)}) custom-call(f32[256,32,128]{2,1,0:T(8,128)} %modes_ref.3, f32[32,128]{1,0:T(8,128)S(1)} %copy-done, f32[264,128]{1,0:T(8,128)S(1)} %get-tuple-element.20.north_ref, f32[264,128]{1,0:T(8,128)S(1)} %get-tuple-element.19.south_ref, ...), custom_call_target="tpu_custom_call" | custom-call | tf_op jit(solution)/shard_map/sums/pallas_call | solution.py:218
  27.3 0.6 copy-done.4
  27.9 0.1 collective-permute-start.4
  28.0 1.4 %collective-permute-done.4 = f32[288,128]{1,0:T(8,128)S(1)} collective-permute-done((f32[288,128]{1,0:T(8,128)S(1)}, f32[288,128]{1,0:T(8,128)S(1)}, u32[]{:S(2)}, u32[]{:S(2)}) %collective-permute-start.4) | collective-permute-done | bytes 147488 | tf_op jit(solution)/shard_map/ppermute | solution.py:243
  29.4 13.6 %all_to_all.15 = f32[16,18,128]{2,1,0:T(8,128)S(1)} all-to-all(f32[16,18,128]{2,1,0:T(8,128)S(1)} %reshape.26), channel_id=1, replica_groups=mesh['x'=4,'core'=2,'z'=8,'y'=4] {'x','y'}, dimensions={0} | all-to-all | bytes 294912 | tf_op jit(solution)/shard_map/all_to_all | solution.py:248
  43.0 14.8 %all_to_all.16 = f32[8,18,128]{2,1,0:T(8,128)S(1)} all-to-all(f32[8,18,128]{2,1,0:T(8,128)S(1)} %broadcast_in_dim.4), channel_id=1, replica_groups=mesh['x'=4,'core'=2,'z'=8,'y'=4] {'z'}, dimensions={0} | all-to-all | bytes 147456 | tf_op jit(solution)/shard_map/all_to_all | solution.py:252
  57.9 10.3 %all_to_all.17 = f32[16,18,128]{2,1,0:T(8,128)S(1)} all-to-all(f32[16,18,128]{2,1,0:T(8,128)S(1)} %broadcast_in_dim.5), channel_id=1, replica_groups=mesh['x'=4,'core'=2,'z'=8,'y'=4] {'x','y'}, dimensions={0} | all-to-all | bytes 294912 | tf_op jit(solution)/shard_map/all_to_all | solution.py:252
  68.1 4.6 %collective-permute-start.5 = (f32[288,128]{1,0:T(8,128)S(1)}, f32[288,128]{1,0:T(8,128)S(1)}, u32[]{:S(2)}, u32[]{:S(2)}) collective-permute-start(f32[288,128]{1,0:T(8,128)S(1)} %reshape.27), channel_id=1, source_target_pairs={{0,32},{32,0},{1,33},{33,1},{2,34},{34,2},{3,35},{35,3},{4,36},{36... | collective-permute-start | bytes 442376 | tf_op jit(solution)/shard_map/ppermute | solution.py:243
  72.7 1.0 %collective-permute-done.5 = f32[288,128]{1,0:T(8,128)S(1)} collective-permute-done((f32[288,128]{1,0:T(8,128)S(1)}, f32[288,128]{1,0:T(8,128)S(1)}, u32[]{:S(2)}, u32[]{:S(2)}) %collective-permute-start.5) | collective-permute-done | bytes 147488 | tf_op jit(solution)/shard_map/ppermute | solution.py:243
  73.8 0.7 pad_maximum_fusion.pack_ref
  74.5 19.4 %finish.1 = (f32[32,128]{1,0:T(8,128)}, f32[256,32,128]{2,1,0:T(8,128)}, f32[256,256]{1,0:T(8,128)}) custom-call(f32[576,128]{1,0:T(8,128)} %pad_maximum_fusion.pack_ref, f32[32,256,128]{2,1,0:T(8,128)} %get-tuple-element.15.adv_hbm, f32[32,128]{1,0:T(8,128)} %copy-done.4), custom_call_target="tpu_custom_call" | custom-call | tf_op jit(solution)/shard_map/finish/pallas_call | solution.py:405
  (24 shorter events, 0.2 us)
Async XLA Ops:
  0.6 18.0 %copy-start = (f32[32,128]{1,0:T(8,128)S(1)}, f32[32,128]{1,0:T(8,128)}, u32[]{:S(2)}) copy-start(f32[32,128]{1,0:T(8,128)} %mean_ref.3) | copy-start | bytes 49156
  0.6 18.0 %copy-start.7 = (f32[1,1,64]{2,1,0:T(1,128)S(1)}, f32[1,1,64]{2,1,0:T(1,128)}, u32[]{:S(2)}) copy-start(f32[1,1,64]{2,1,0:T(1,128)} %param.15) | copy-start | bytes 772
  0.7 18.0 %copy-start.6 = (f32[1,1,64]{2,1,0:T(1,128)S(1)}, f32[1,1,64]{2,1,0:T(1,128)}, u32[]{:S(2)}) copy-start(f32[1,1,64]{2,1,0:T(1,128)} %param.14) | copy-start | bytes 772
  0.7 18.0 %copy-start.5 = (s32[1,1,64]{2,1,0:T(1,128)S(1)}, s32[1,1,64]{2,1,0:T(1,128)}, u32[]{:S(2)}) copy-start(s32[1,1,64]{2,1,0:T(1,128)} %param.13) | copy-start | bytes 772
  0.7 18.0 %copy-start.3 = (s32[32,128]{1,0:T(8,128)S(1)}, s32[32,128]{1,0:T(8,128)}, u32[]{:S(2)}) copy-start(s32[32,128]{1,0:T(8,128)} %mask_ref.1) | copy-start | bytes 49156
  0.7 18.0 %copy-start.2 = (f32[32,128]{1,0:T(8,128)S(1)}, f32[32,128]{1,0:T(8,128)}, u32[]{:S(2)}) copy-start(f32[32,128]{1,0:T(8,128)} %vvel_ref.1) | copy-start | bytes 49156
  0.7 18.0 %copy-start.1 = (f32[32,128]{1,0:T(8,128)S(1)}, f32[32,128]{1,0:T(8,128)}, u32[]{:S(2)}) copy-start(f32[32,128]{1,0:T(8,128)} %uvel_ref.1) | copy-start | bytes 49156
  5.3 10.8 %collective-permute-start.3 = (f32[96,128]{1,0:T(8,128)S(1)}, f32[96,128]{1,0:T(8,128)S(1)}, u32[]{:S(2)}, u32[]{:S(2)}) collective-permute-start(f32[96,128]{1,0:T(8,128)S(1)} %get-tuple-element.25), channel_id=1, source_target_pairs={{1,2},{3,4},{5,6},{7,8},{9,10},{11,12},{13,14},{15,16},{17,18},{19... | collective-permute-start | bytes 147464 | tf_op jit(solution)/shard_map/ppermute | solution.py:243
  5.9 10.1 %collective-permute-start.2 = (f32[96,128]{1,0:T(8,128)S(1)}, f32[96,128]{1,0:T(8,128)S(1)}, u32[]{:S(2)}, u32[]{:S(2)}) collective-permute-start(f32[96,128]{1,0:T(8,128)S(1)} %get-tuple-element.26), channel_id=1, source_target_pairs={{0,1},{2,3},{4,5},{6,7},{8,9},{10,11},{12,13},{14,15},{16,17},{18,... | collective-permute-start | bytes 147464 | tf_op jit(solution)/shard_map/ppermute | solution.py:243
  11.7 6.9 %collective-permute-start.1 = (f32[264,128]{1,0:T(8,128)S(1)}, f32[264,128]{1,0:T(8,128)S(1)}, u32[]{:S(2)}, u32[]{:S(2)}) collective-permute-start(f32[264,128]{1,0:T(8,128)S(1)} %get-tuple-element.21), channel_id=1, source_target_pairs={{32,64},{96,128},{160,192},{64,32},{128,96},{192,160},{33,65},{97,... | collective-permute-start | bytes 405512 | tf_op jit(solution)/shard_map/ppermute | solution.py:243
  15.9 2.7 %collective-permute-start = (f32[264,128]{1,0:T(8,128)S(1)}, f32[264,128]{1,0:T(8,128)S(1)}, u32[]{:S(2)}, u32[]{:S(2)}) collective-permute-start(f32[264,128]{1,0:T(8,128)S(1)} %get-tuple-element.22), channel_id=1, source_target_pairs={{0,32},{64,96},{128,160},{192,224},{32,0},{96,64},{160,128},{224,1... | collective-permute-start | bytes 405512 | tf_op jit(solution)/shard_map/ppermute | solution.py:243
  27.3 0.6 copy-start.4
  27.9 1.5 %collective-permute-start.4 = (f32[288,128]{1,0:T(8,128)S(1)}, f32[288,128]{1,0:T(8,128)S(1)}, u32[]{:S(2)}, u32[]{:S(2)}) collective-permute-start(f32[288,128]{1,0:T(8,128)S(1)} %slice_select_fusion), channel_id=1, source_target_pairs={{0,32},{32,0},{1,33},{33,1},{2,34},{34,2},{3,35},{35,3},{4,36},{36... | collective-permute-start | bytes 442376 | tf_op jit(solution)/shard_map/ppermute | solution.py:243
  68.1 5.6 %collective-permute-start.5 = (f32[288,128]{1,0:T(8,128)S(1)}, f32[288,128]{1,0:T(8,128)S(1)}, u32[]{:S(2)}, u32[]{:S(2)}) collective-permute-start(f32[288,128]{1,0:T(8,128)S(1)} %reshape.27), channel_id=1, source_target_pairs={{0,32},{32,0},{1,33},{33,1},{2,34},{34,2},{3,35},{35,3},{4,36},{36... | collective-permute-start | bytes 442376 | tf_op jit(solution)/shard_map/ppermute | solution.py:243

commit v4 on v3

--- a/solution.py
+++ b/solution.py
@@ -47,7 +47,14 @@
     return copies
 
 
-def edges_kernel(modes_ref, mean_ref, low_ref, high_ref, west_ref, east_ref, block, in_sem, mean_sem):
+def odd_sides():
+    return lax.axis_index("core") == 1, lax.axis_index("y") % 2 == 1
+
+
+def edges_kernel(
+    modes_ref, mean_ref, lat_one, lat_two, lon_one, lon_two,
+    low_ref, high_ref, west_ref, east_ref, block, in_sem, mean_sem,
+):
     chunks, rows, lats, lons = block.shape
     groups = lons // lats
     total = chunks * rows
@@ -83,6 +90,13 @@
         copy.wait()
     low_ref[total : total + 8] = jnp.broadcast_to(west_ref[packed : packed + 1], (8, lons))
     high_ref[total : total + 8] = jnp.broadcast_to(west_ref[packed + lats - 1 : packed + lats], (8, lons))
+    odd_lat, odd_lon = odd_sides()
+    for odd, below, above, one, two in (
+        (odd_lat, low_ref, high_ref, lat_one, lat_two),
+        (odd_lon, west_ref, east_ref, lon_one, lon_two),
+    ):
+        one[...] = jnp.where(odd, below[...], above[...])
+        two[...] = jnp.where(odd, above[...], below[...])
 
 
 def edges_of(modes, mean_state):
@@ -95,12 +109,13 @@
         in_specs=[HBM] * 2,
         out_specs=[VMEM] * 4,
         out_shape=[jax.ShapeDtypeStruct(s, jnp.float32) for s in sides],
-        scratch_shapes=[
+        scratch_shapes=[pltpu.VMEM(s, jnp.float32) for s in sides]
+        + [
             pltpu.VMEM((chunks, count // chunks, lats, lons), jnp.float32),
             pltpu.SemaphoreType.DMA((chunks,)),
             pltpu.SemaphoreType.DMA((2,)),
         ],
-        compiler_params=room(61),
+        compiler_params=room(50),
         name="edges",
     )(modes, mean_state)
 
@@ -115,11 +130,21 @@
 
 
 def sums_kernel(
-    modes_ref, mean_ref, north_ref, south_ref, east_ref, west_ref, uvel_ref, vvel_ref, mask_ref,
-    index_ref, value_ref, weight_ref, adv_hbm, fore_ref, pack_ref, slab_ref, adv_ref, coef, parts, seen, out_sem,
+    modes_hbm, mean_ref, lat_one, lat_two, lon_one, lon_two, uvel_ref, vvel_ref, mask_ref,
+    index_ref, value_ref, weight_ref, adv_hbm, keep_ref, send_ref,
+    block, slab_ref, adv_ref, north_ref, south_ref, east_ref, west_ref, pack_ref, coef, parts, seen,
+    in_sem, out_sem,
 ):
     lats, count, lons = slab_ref.shape
-    chunks = out_sem.shape[0]
+    reads = reads_of(modes_hbm, block, in_sem)
+    odd_lat, odd_lon = odd_sides()
+    for odd, below, above, one, two in (
+        (odd_lat, south_ref, north_ref, lat_one, lat_two),
+        (odd_lon, west_ref, east_ref, lon_one, lon_two),
+    ):
+        above[...] = jnp.where(odd, two[...], one[...])
+        below[...] = jnp.where(odd, one[...], two[...])
+    chunks = out_sem.shape[0] - 1
     deep = lats // chunks
     writes = []
     for i in range(chunks):
@@ -127,10 +152,6 @@
         writes.append(pltpu.make_async_copy(adv_ref.at[span], adv_hbm.at[span], out_sem.at[i]))
     groups = lons // lats
     rows = count // groups
-    for r in range(0, count, rows):
-        for lat in range(0, lats, 8):
-            for e, line in enumerate(by_latitude(modes_ref.at[r : r + rows], lat)):
-                slab_ref[lat + e, r : r + rows, :] = line
     sea = mask_ref[...].astype(jnp.float32)
     half_u, half_v = 0.5 * uvel_ref[...], 0.5 * vvel_ref[...]
     coef[0] = sea * 0.2
@@ -146,7 +167,16 @@
     northern = jnp.concatenate([mean[1:], north_ref[count : count + 1]], axis=0)
     southern = jnp.concatenate([south_ref[count : count + 1], mean[:-1]], axis=0)
     fore = coef[0] * mean + coef[1] * eastern + coef[2] * western
+    fore_ref = adv_ref.at[lats, 0:lats]
     fore_ref[...] = fore + coef[3] * northern + coef[4] * southern
+    writes.append(pltpu.make_async_copy(fore_ref, adv_hbm.at[lats, 0:lats], out_sem.at[chunks]))
+    writes[-1].start()
+    for i, copy in enumerate(reads):
+        copy.wait()
+        part = block.shape[1]
+        for lat in range(0, lats, 8):
+            for e, line in enumerate(by_latitude(block.at[i], lat)):
+                slab_ref[lat + e, i * part : (i + 1) * part, :] = line
 
     first = lanes_of((rows, lons)) == 0
     last = lanes_of((rows, lons)) == lons - 1
@@ -208,6 +238,9 @@
     for i, line in enumerate((diag_c, obs_b[0:1])):
         pack_ref[2 * count + 2 * i : 2 * count + 2 * i + 1] = line[:, 0:lons]
         pack_ref[2 * count + 2 * i + 1 : 2 * count + 2 * i + 2] = line[:, lons:]
+    half = PACK // 2
+    keep_ref[...] = jnp.where(odd_lat, pack_ref[half:], pack_ref[:half])
+    send_ref[...] = jnp.where(odd_lat, pack_ref[:half], pack_ref[half:])
     for copy in writes:
         copy.wait()
 
@@ -217,20 +250,23 @@
     line = lambda x: x.reshape(1, -1)
     return pl.pallas_call(
         sums_kernel,
-        in_specs=[VMEM] * 12,
+        in_specs=[HBM] + [VMEM] * 11,
         out_specs=[HBM] + [VMEM] * 2,
-        out_shape=[
-            jax.ShapeDtypeStruct((lats, count, lons), jnp.float32),
-            jax.ShapeDtypeStruct((lats, lons), jnp.float32),
-            jax.ShapeDtypeStruct((PACK, lons), jnp.float32),
-        ],
+        out_shape=[jax.ShapeDtypeStruct((lats + 1, count, lons), jnp.float32)]
+        + [jax.ShapeDtypeStruct((PACK // 2, lons), jnp.float32)] * 2,
         scratch_shapes=[
+            pltpu.VMEM((8, count // 8, lats, lons), jnp.float32),
             pltpu.VMEM((lats, count, lons), jnp.float32),
-            pltpu.VMEM((lats, count, lons), jnp.float32),
+            pltpu.VMEM((lats + 1, count, lons), jnp.float32),
+        ]
+        + [pltpu.VMEM(side.shape, jnp.float32) for side in sides]
+        + [
+            pltpu.VMEM((PACK, lons), jnp.float32),
             pltpu.VMEM((5, lats, lons), jnp.float32),
             pltpu.VMEM((2, count, count), jnp.float32),
             pltpu.VMEM((count, obs_index.size), jnp.float32),
             pltpu.SemaphoreType.DMA((8,)),
+            pltpu.SemaphoreType.DMA((9,)),
         ],
         compiler_params=room(50),
         name="sums",
@@ -252,16 +288,12 @@
     return lax.all_to_all(jnp.broadcast_to(value[None], (lax.axis_size(axes),) + value.shape), axes, 0, 0)
 
 
-def sum_everywhere(value):
-    half = value.shape[0] // 2
-    low, high = value[:half], value[half:]
-    upper = lax.axis_index("core") == 1
-    value = jnp.where(upper, high, low) + swap(jnp.where(upper, low, high), "core", 0)
+def sum_everywhere(keep, send):
+    value = keep + swap(send, "core", 0)
     value = scatter_sum(value, ("x", "y"))
     value = gather(value, "z").sum(0)
-    value = gather(value, ("x", "y")).reshape(half, LANES)
-    other = swap(value, "core", 0)
-    return jnp.concatenate([jnp.where(upper, other, value), jnp.where(upper, value, other)])
+    value = gather(value, ("x", "y")).reshape(keep.shape)
+    return value, swap(value, "core", 0)
 
 
 def factor_panels(work, upper, inverse):
@@ -349,11 +381,11 @@
 
 
 def finish_kernel(
-    scale, pack_ref, adv_hbm, fore_ref, mean_ref, basis_hbm, root_hbm,
-    work, upper, inverse, root, adv, basis, in_sem, out_sem, root_sem,
+    scale, mine_ref, other_ref, adv_hbm, mean_ref, basis_hbm, root_hbm,
+    pack_ref, work, upper, inverse, root, adv, basis, in_sem, out_sem, root_sem,
 ):
-    lats, size, lons = adv.shape
-    steps = in_sem.shape[0]
+    lats, size, lons = adv.shape[0] - 1, adv.shape[1], adv.shape[2]
+    steps = out_sem.shape[0]
     deep = lats // steps
     reads, writes = [], []
     for i in range(steps):
@@ -361,6 +393,12 @@
         reads.append(pltpu.make_async_copy(adv_hbm.at[span], adv.at[span], in_sem.at[i]))
         writes.append(pltpu.make_async_copy(basis.at[i], basis_hbm.at[:, span, :], out_sem.at[i]))
         reads[i].start()
+    fore_ref = adv.at[lats, 0:lats]
+    reads.append(pltpu.make_async_copy(adv_hbm.at[lats, 0:lats], fore_ref, in_sem.at[steps]))
+    reads[steps].start()
+    odd, half = odd_sides()[0], PACK // 2
+    pack_ref[:half] = jnp.where(odd, other_ref[...], mine_ref[...])
+    pack_ref[half:] = jnp.where(odd, mine_ref[...], other_ref[...])
     row = lax.broadcasted_iota(jnp.int32, (size, size), 0)
     col = lax.broadcasted_iota(jnp.int32, (size, size), 1)
     eye = row == col
@@ -380,6 +418,7 @@
     half = high_dot(jnp.broadcast_to(line(2), (8, size)), finv, ((1,), (1,)))
     coef = high_dot(half, finv, ((1,), (0,))) / (size - 1.0)
     left = jnp.concatenate([inverse[0] * (q_row * scale), coef], axis=0)
+    reads[steps].wait()
     for i in range(steps):
         reads[i].wait()
         wide = jnp.concatenate([adv[i * deep + e] for e in range(deep)], axis=1)
@@ -398,49 +437,45 @@
         copy.wait()
 
 
-def finish(pack, advanced, fore, scale):
-    lats, size, lons = advanced.shape
+def finish(mine, other, advanced, scale):
+    lats, size, lons = advanced.shape[0] - 1, advanced.shape[1], advanced.shape[2]
     steps = 4
     square = (size, size)
     return pl.pallas_call(
         functools.partial(finish_kernel, scale),
-        in_specs=[VMEM, HBM, VMEM],
+        in_specs=[VMEM, VMEM, HBM],
         out_specs=[VMEM, HBM, HBM],
         out_shape=[
             jax.ShapeDtypeStruct((lats, lons), jnp.float32),
             jax.ShapeDtypeStruct((size, lats, lons), jnp.float32),
             jax.ShapeDtypeStruct(square, jnp.float32),
         ],
-        scratch_shapes=[pltpu.VMEM((2,) + square, jnp.float32)] * 3
+        scratch_shapes=[pltpu.VMEM((PACK, lons), jnp.float32)]
+        + [pltpu.VMEM((2,) + square, jnp.float32)] * 3
         + [
             pltpu.VMEM(square, jnp.float32),
-            pltpu.VMEM((lats, size, lons), jnp.float32),
+            pltpu.VMEM((lats + 1, size, lons), jnp.float32),
             pltpu.VMEM((steps, size, lats // steps, lons), jnp.float32),
-            pltpu.SemaphoreType.DMA((steps,)),
+            pltpu.SemaphoreType.DMA((steps + 1,)),
             pltpu.SemaphoreType.DMA((steps,)),
             pltpu.SemaphoreType.DMA,
         ],
-        compiler_params=room(61),
+        compiler_params=room(50),
         name="finish",
-    )(pack, advanced, fore)
+    )(mine, other, advanced)
 
 
 def body(mean_state, modes, east_vel, north_vel, sea_mask, obs_index, obs_value, obs_weight):
     count, lat_rows, lon_cols = modes.shape
-    low, high, west, east = edges_of(modes, mean_state)
+    lat_one, lat_two, lon_one, lon_two = edges_of(modes, mean_state)
     band, tile = ("x", "core"), ("z", "y")
-    sides = []
-    for axis, first, last in ((band, low, high), (tile, west, east)):
-        even = lax.axis_index(axis) % 2 == 0
-        one = swap(jnp.where(even, last, first), axis, 0)
-        two = swap(jnp.where(even, first, last), axis, 1)
-        sides += [jnp.where(even, one, two), jnp.where(even, two, one)]
-    advanced, fore, pack = sums_of(
+    sides = [swap(lat_one, band, 0), swap(lat_two, band, 1), swap(lon_one, tile, 0), swap(lon_two, tile, 1)]
+    advanced, keep, send = sums_of(
         modes, mean_state, sides, east_vel, north_vel, sea_mask, obs_index, obs_value, obs_weight
     )
-    pack = sum_everywhere(pack)
+    mine, other = sum_everywhere(keep, send)
     points = lat_rows * lon_cols * lax.axis_size(band) * lax.axis_size(tile)
-    mean_analysis, basis, root_factor = finish(pack, advanced, fore, float(points) ** 0.5)
+    mean_analysis, basis, root_factor = finish(mine, other, advanced, float(points) ** 0.5)
     return (mean_analysis, basis, root_factor)
 
 

time: 94.4 us -> 91.7 us (0.971)
  blocking collectives: 38.6 us -> 42.5 us
  starting transfers between devices: 14.4 us -> 11.3 us
  other arithmetic: 2.69 us -> 0.05 us
  Pallas kernels: 31.6 us -> 30.4 us
    ppermute x6, starting transfers between devices: 14.4 us -> 11.3 us  [swap(): return lax.ppermute(value, axis, pairs)]
    all_to_all x1, blocking collectives: 13.6 us -> 16.5 us  [scatter_sum(): return lax.all_to_all(value.reshape(count, -1, LANES), axes, 0, 0).sum(0)]
    select_n x6 -> x0, other arithmetic: 1.9 us -> none  [the longest x2 1.82 us: body(): two = swap(jnp.where(even, first, last), axis, 1)]
  transfers between devices with their start and end apart: 6 -> 6, of which waited for: 3 -> 4; matrix products, arithmetic and copies ran while one was open for 1% -> 0% of each run, Pallas kernels for 0% -> 0%
where the time goes in v4:
time: 91.7 us; the launch traced here: 91.3 us
  blocking collectives  42.5 us (46%)
  Pallas kernels  30.4 us (33%)
  starting transfers between devices  11.3 us (12%)
  waiting for transfers between devices  5.35 us (6%)
  between operations  0.95 us (1%)
    all_to_all x2, blocking collectives, gather(): lax.all_to_all(jnp.broadcast_to(value[None], (lax.axis_size(axes),) + val...  26 us
    pallas_call x1, Pallas kernels, finish(): pl.pallas_call(functools.partial(finish_kernel, scale), in_specs=[VMEM, V...  19.2 us
    all_to_all x1, blocking collectives, scatter_sum(): return lax.all_to_all(value.reshape(count, -1, LANES), axes, 0, 0).sum(0)  16.5 us
    ppermute x6, starting transfers between devices, swap(): return lax.ppermute(value, axis, pairs)  11.3 us
    pallas_call x1, Pallas kernels, sums_of(): pl.pallas_call(sums_kernel, in_specs=[HBM] + [VMEM] * 11, out_specs=[HBM]...  8.19 us
    ppermute x6, waiting for transfers between devices, swap(): return lax.ppermute(value, axis, pairs)  5.35 us
    pallas_call x1, Pallas kernels, edges_of(): pl.pallas_call(edges_kernel, in_specs=[HBM] * 2, out_specs=[VMEM] * 4, ou...  3.04 us
  transfers between devices with their start and end apart: 6, of which 4 were waited for; matrix products, arithmetic and copies ran while one was open for 0% of the time, Pallas kernels for 0%

profile of v4, /device:TPU:1, one launch (start us, length us, event | category | flops | bytes accessed | tf_op | source)
XLA Modules:
  0.0 91.3 jit_solution(553892539422913017)
XLA Ops:
  0.6 0.0 copy-start
  0.6 0.7 copy-done
  1.4 0.0 copy-start.5
  1.4 0.0 copy-start.6
  1.4 3.0 %edges.1 = (f32[264,128]{1,0:T(8,128)S(1)}, f32[264,128]{1,0:T(8,128)S(1)}, f32[96,128]{1,0:T(8,128)S(1)}, f32[96,128]{1,0:T(8,128)S(1)}) custom-call(f32[256,32,128]{2,1,0:T(8,128)} %modes_hbm.1, f32[32,128]{1,0:T(8,128)S(1)} %copy-done), custom_call_target="tpu_custom_call" | custom-call | tf_op jit(solution)/shard_map/edges/pallas_call | solution.py:107
  4.4 3.3 %collective-permute-start = (f32[264,128]{1,0:T(8,128)S(1)}, f32[264,128]{1,0:T(8,128)S(1)}, u32[]{:S(2)}, u32[]{:S(2)}) collective-permute-start(f32[264,128]{1,0:T(8,128)S(1)} %get-tuple-element.10), channel_id=1, source_target_pairs={{0,32},{64,96},{128,160},{192,224},{32,0},{96,64},{160,128},{224,1... | collective-permute-start | bytes 405512 | tf_op jit(solution)/shard_map/ppermute | solution.py:279
  7.8 1.9 %collective-permute-start.1 = (f32[264,128]{1,0:T(8,128)S(1)}, f32[264,128]{1,0:T(8,128)S(1)}, u32[]{:S(2)}, u32[]{:S(2)}) collective-permute-start(f32[264,128]{1,0:T(8,128)S(1)} %get-tuple-element.11), channel_id=1, source_target_pairs={{32,64},{96,128},{160,192},{64,32},{128,96},{192,160},{33,65},{97,... | collective-permute-start | bytes 405512 | tf_op jit(solution)/shard_map/ppermute | solution.py:279
  9.7 0.8 collective-permute-start.2
  10.4 0.7 collective-permute-start.3
  11.1 1.6 %collective-permute-done.2.lon_one = f32[96,128]{1,0:T(8,128)S(1)} collective-permute-done((f32[96,128]{1,0:T(8,128)S(1)}, f32[96,128]{1,0:T(8,128)S(1)}, u32[]{:S(2)}, u32[]{:S(2)}) %collective-permute-start.2) | collective-permute-done | bytes 49184 | tf_op jit(solution)/shard_map/ppermute | solution.py:279
  12.7 0.0 collective-permute-done.3.lon_two
  12.7 0.0 collective-permute-done.lat_one
  12.7 1.4 %collective-permute-done.1.lat_two = f32[264,128]{1,0:T(8,128)S(1)} collective-permute-done((f32[264,128]{1,0:T(8,128)S(1)}, f32[264,128]{1,0:T(8,128)S(1)}, u32[]{:S(2)}, u32[]{:S(2)}) %collective-permute-start.1) | collective-permute-done | bytes 135200 | tf_op jit(solution)/shard_map/ppermute | solution.py:279
  14.1 0.0 copy-done.1
  14.1 0.0 copy-done.2
  14.1 8.2 %sums.1 = (f32[33,256,128]{2,1,0:T(8,128)}, f32[288,128]{1,0:T(8,128)S(1)}, f32[288,128]{1,0:T(8,128)S(1)}) custom-call(f32[256,32,128]{2,1,0:T(8,128)} %modes_hbm.1, f32[32,128]{1,0:T(8,128)S(1)} %copy-done, f32[264,128]{1,0:T(8,128)S(1)} %collective-permute-done.lat_one, f32[264,128]{1,0:T(8,128)S(1)} %collective-permute-done.1.lat_two, ...), custom_call_target="tpu_custom_call" | custom-call | tf_op jit(solution)/shard_map/sums/pallas_call | solution.py:251
  22.3 0.1 collective-permute-start.4
  22.4 1.4 %collective-permute-done.4 = f32[288,128]{1,0:T(8,128)S(1)} collective-permute-done((f32[288,128]{1,0:T(8,128)S(1)}, f32[288,128]{1,0:T(8,128)S(1)}, u32[]{:S(2)}, u32[]{:S(2)}) %collective-permute-start.4) | collective-permute-done | bytes 147488 | tf_op jit(solution)/shard_map/ppermute | solution.py:279
  23.8 16.5 %all_to_all.15 = f32[16,18,128]{2,1,0:T(8,128)S(1)} all-to-all(f32[16,18,128]{2,1,0:T(8,128)S(1)} %reshape.26), channel_id=1, replica_groups=mesh['x'=4,'core'=2,'z'=8,'y'=4] {'x','y'}, dimensions={0} | all-to-all | bytes 294912 | tf_op jit(solution)/shard_map/all_to_all | solution.py:284
  40.4 15.7 %all_to_all.16 = f32[8,18,128]{2,1,0:T(8,128)S(1)} all-to-all(f32[8,18,128]{2,1,0:T(8,128)S(1)} %broadcast_in_dim.4), channel_id=1, replica_groups=mesh['x'=4,'core'=2,'z'=8,'y'=4] {'z'}, dimensions={0} | all-to-all | bytes 147456 | tf_op jit(solution)/shard_map/all_to_all | solution.py:288
  56.1 10.3 %all_to_all.17 = f32[16,18,128]{2,1,0:T(8,128)S(1)} all-to-all(f32[16,18,128]{2,1,0:T(8,128)S(1)} %broadcast_in_dim.5), channel_id=1, replica_groups=mesh['x'=4,'core'=2,'z'=8,'y'=4] {'x','y'}, dimensions={0} | all-to-all | bytes 294912 | tf_op jit(solution)/shard_map/all_to_all | solution.py:288
  66.4 4.6 %collective-permute-start.5 = (f32[288,128]{1,0:T(8,128)S(1)}, f32[288,128]{1,0:T(8,128)S(1)}, u32[]{:S(2)}, u32[]{:S(2)}) collective-permute-start(f32[288,128]{1,0:T(8,128)S(1)} %reshape.27.mine_ref), channel_id=1, source_target_pairs={{0,32},{32,0},{1,33},{33,1},{2,34},{34,2},{3,35},{35,3},{4,36},{36... | collective-permute-start | bytes 442376 | tf_op jit(solution)/shard_map/ppermute | solution.py:279
  71.0 1.0 %collective-permute-done.5.other_ref = f32[288,128]{1,0:T(8,128)S(1)} collective-permute-done((f32[288,128]{1,0:T(8,128)S(1)}, f32[288,128]{1,0:T(8,128)S(1)}, u32[]{:S(2)}, u32[]{:S(2)}) %collective-permute-start.5) | collective-permute-done | bytes 147488 | tf_op jit(solution)/shard_map/ppermute | solution.py:279
  72.0 19.2 %finish.1 = (f32[32,128]{1,0:T(8,128)}, f32[256,32,128]{2,1,0:T(8,128)}, f32[256,256]{1,0:T(8,128)}) custom-call(f32[288,128]{1,0:T(8,128)S(1)} %reshape.27.mine_ref, f32[288,128]{1,0:T(8,128)S(1)} %collective-permute-done.5.other_ref, f32[33,256,128]{2,1,0:T(8,128)} %get-tuple-element.16.adv_hbm), custom_call_target="tpu_custom_call" | custom-call | tf_op jit(solution)/shard_map/finish/pallas_call | solution.py:444
  (15 shorter events, 0.1 us)
Async XLA Ops:
  0.6 0.7 copy-start
  1.4 12.7 %copy-start.1 = (f32[32,128]{1,0:T(8,128)S(1)}, f32[32,128]{1,0:T(8,128)}, u32[]{:S(2)}) copy-start(f32[32,128]{1,0:T(8,128)} %uvel_ref.1) | copy-start | bytes 49156
  1.4 12.7 %copy-start.2 = (f32[32,128]{1,0:T(8,128)S(1)}, f32[32,128]{1,0:T(8,128)}, u32[]{:S(2)}) copy-start(f32[32,128]{1,0:T(8,128)} %vvel_ref.1) | copy-start | bytes 49156
  1.4 12.7 %copy-start.3 = (s32[32,128]{1,0:T(8,128)S(1)}, s32[32,128]{1,0:T(8,128)}, u32[]{:S(2)}) copy-start(s32[32,128]{1,0:T(8,128)} %mask_ref.1) | copy-start | bytes 49156
  1.4 12.7 %copy-start.4 = (s32[1,1,64]{2,1,0:T(1,128)S(1)}, s32[1,1,64]{2,1,0:T(1,128)}, u32[]{:S(2)}) copy-start(s32[1,1,64]{2,1,0:T(1,128)} %param.13) | copy-start | bytes 772
  1.4 12.7 %copy-start.5 = (f32[1,1,64]{2,1,0:T(1,128)S(1)}, f32[1,1,64]{2,1,0:T(1,128)}, u32[]{:S(2)}) copy-start(f32[1,1,64]{2,1,0:T(1,128)} %param.14) | copy-start | bytes 772
  1.4 12.7 %copy-start.6 = (f32[1,1,64]{2,1,0:T(1,128)S(1)}, f32[1,1,64]{2,1,0:T(1,128)}, u32[]{:S(2)}) copy-start(f32[1,1,64]{2,1,0:T(1,128)} %param.15) | copy-start | bytes 772
  4.4 8.3 %collective-permute-start = (f32[264,128]{1,0:T(8,128)S(1)}, f32[264,128]{1,0:T(8,128)S(1)}, u32[]{:S(2)}, u32[]{:S(2)}) collective-permute-start(f32[264,128]{1,0:T(8,128)S(1)} %get-tuple-element.10), channel_id=1, source_target_pairs={{0,32},{64,96},{128,160},{192,224},{32,0},{96,64},{160,128},{224,1... | collective-permute-start | bytes 405512 | tf_op jit(solution)/shard_map/ppermute | solution.py:279
  7.8 6.3 %collective-permute-start.1 = (f32[264,128]{1,0:T(8,128)S(1)}, f32[264,128]{1,0:T(8,128)S(1)}, u32[]{:S(2)}, u32[]{:S(2)}) collective-permute-start(f32[264,128]{1,0:T(8,128)S(1)} %get-tuple-element.11), channel_id=1, source_target_pairs={{32,64},{96,128},{160,192},{64,32},{128,96},{192,160},{33,65},{97,... | collective-permute-start | bytes 405512 | tf_op jit(solution)/shard_map/ppermute | solution.py:279
  9.7 3.0 %collective-permute-start.2 = (f32[96,128]{1,0:T(8,128)S(1)}, f32[96,128]{1,0:T(8,128)S(1)}, u32[]{:S(2)}, u32[]{:S(2)}) collective-permute-start(f32[96,128]{1,0:T(8,128)S(1)} %get-tuple-element.12), channel_id=1, source_target_pairs={{0,1},{2,3},{4,5},{6,7},{8,9},{10,11},{12,13},{14,15},{16,17},{18,... | collective-permute-start | bytes 147464 | tf_op jit(solution)/shard_map/ppermute | solution.py:279
  10.4 2.3 %collective-permute-start.3 = (f32[96,128]{1,0:T(8,128)S(1)}, f32[96,128]{1,0:T(8,128)S(1)}, u32[]{:S(2)}, u32[]{:S(2)}) collective-permute-start(f32[96,128]{1,0:T(8,128)S(1)} %get-tuple-element.13), channel_id=1, source_target_pairs={{1,2},{3,4},{5,6},{7,8},{9,10},{11,12},{13,14},{15,16},{17,18},{19... | collective-permute-start | bytes 147464 | tf_op jit(solution)/shard_map/ppermute | solution.py:279
  22.3 1.5 %collective-permute-start.4 = (f32[288,128]{1,0:T(8,128)S(1)}, f32[288,128]{1,0:T(8,128)S(1)}, u32[]{:S(2)}, u32[]{:S(2)}) collective-permute-start(f32[288,128]{1,0:T(8,128)S(1)} %get-tuple-element.15), channel_id=1, source_target_pairs={{0,32},{32,0},{1,33},{33,1},{2,34},{34,2},{3,35},{35,3},{4,36},{36... | collective-permute-start | bytes 442376 | tf_op jit(solution)/shard_map/ppermute | solution.py:279
  66.4 5.6 %collective-permute-start.5 = (f32[288,128]{1,0:T(8,128)S(1)}, f32[288,128]{1,0:T(8,128)S(1)}, u32[]{:S(2)}, u32[]{:S(2)}) collective-permute-start(f32[288,128]{1,0:T(8,128)S(1)} %reshape.27.mine_ref), channel_id=1, source_target_pairs={{0,32},{32,0},{1,33},{33,1},{2,34},{34,2},{3,35},{35,3},{4,36},{36... | collective-permute-start | bytes 442376 | tf_op jit(solution)/shard_map/ppermute | solution.py:279

commit v5 on v4

--- a/solution.py
+++ b/solution.py
@@ -120,6 +120,33 @@
     )(modes, mean_state)
 
 
+def slabs_kernel(modes_ref, slab_ref, block, in_sem):
+    chunks, rows, lats, lons = block.shape
+    for i, copy in enumerate(reads_of(modes_ref, block, in_sem)):
+        copy.wait()
+        for first in range(0, lats, 8):
+            for e, line in enumerate(by_latitude(block.at[i], first)):
+                slab_ref[first + e, i * rows : (i + 1) * rows, :] = line
+
+
+def slabs_of(modes):
+    count, lats, lons = modes.shape
+    chunks = 8
+    return pl.pallas_call(
+        slabs_kernel,
+        in_specs=[HBM],
+        out_specs=VMEM,
+        out_shape=jax.ShapeDtypeStruct((lats, count, lons), jnp.float32),
+        scratch_shapes=[
+            pltpu.VMEM((chunks, count // chunks, lats, lons), jnp.float32),
+            pltpu.SemaphoreType.DMA((chunks,)),
+        ],
+        compiler_params=room(24),
+        cost_estimate=pl.CostEstimate(flops=2**22, bytes_accessed=2 * modes.size * 4, transcendentals=0),
+        name="slabs",
+    )(modes)
+
+
 def split(value):
     top = value.astype(jnp.bfloat16)
     return top, (value - top.astype(jnp.float32)).astype(jnp.bfloat16)
@@ -130,13 +157,12 @@
 
 
 def sums_kernel(
-    modes_hbm, mean_ref, lat_one, lat_two, lon_one, lon_two, uvel_ref, vvel_ref, mask_ref,
+    slab_ref, mean_ref, lat_one, lat_two, lon_one, lon_two, uvel_ref, vvel_ref, mask_ref,
     index_ref, value_ref, weight_ref, adv_hbm, keep_ref, send_ref,
-    block, slab_ref, adv_ref, north_ref, south_ref, east_ref, west_ref, pack_ref, coef, parts, seen,
-    in_sem, out_sem,
+    adv_ref, north_ref, south_ref, east_ref, west_ref, pack_ref, coef, parts, seen,
+    out_sem,
 ):
     lats, count, lons = slab_ref.shape
-    reads = reads_of(modes_hbm, block, in_sem)
     odd_lat, odd_lon = odd_sides()
     for odd, below, above, one, two in (
         (odd_lat, south_ref, north_ref, lat_one, lat_two),
@@ -171,12 +197,6 @@
     fore_ref[...] = fore + coef[3] * northern + coef[4] * southern
     writes.append(pltpu.make_async_copy(fore_ref, adv_hbm.at[lats, 0:lats], out_sem.at[chunks]))
     writes[-1].start()
-    for i, copy in enumerate(reads):
-        copy.wait()
-        part = block.shape[1]
-        for lat in range(0, lats, 8):
-            for e, line in enumerate(by_latitude(block.at[i], lat)):
-                slab_ref[lat + e, i * part : (i + 1) * part, :] = line
 
     first = lanes_of((rows, lons)) == 0
     last = lanes_of((rows, lons)) == lons - 1
@@ -245,18 +265,16 @@
         copy.wait()
 
 
-def sums_of(modes, mean_state, sides, east_vel, north_vel, sea_mask, obs_index, obs_value, obs_weight):
-    count, lats, lons = modes.shape
+def sums_of(slabs, mean_state, sides, east_vel, north_vel, sea_mask, obs_index, obs_value, obs_weight):
+    lats, count, lons = slabs.shape
     line = lambda x: x.reshape(1, -1)
     return pl.pallas_call(
         sums_kernel,
-        in_specs=[HBM] + [VMEM] * 11,
+        in_specs=[VMEM] * 12,
         out_specs=[HBM] + [VMEM] * 2,
         out_shape=[jax.ShapeDtypeStruct((lats + 1, count, lons), jnp.float32)]
         + [jax.ShapeDtypeStruct((PACK // 2, lons), jnp.float32)] * 2,
         scratch_shapes=[
-            pltpu.VMEM((8, count // 8, lats, lons), jnp.float32),
-            pltpu.VMEM((lats, count, lons), jnp.float32),
             pltpu.VMEM((lats + 1, count, lons), jnp.float32),
         ]
         + [pltpu.VMEM(side.shape, jnp.float32) for side in sides]
@@ -265,12 +283,11 @@
             pltpu.VMEM((5, lats, lons), jnp.float32),
             pltpu.VMEM((2, count, count), jnp.float32),
             pltpu.VMEM((count, obs_index.size), jnp.float32),
-            pltpu.SemaphoreType.DMA((8,)),
             pltpu.SemaphoreType.DMA((9,)),
         ],
-        compiler_params=room(50),
+        compiler_params=room(47),
         name="sums",
-    )(modes, mean_state, *sides, east_vel, north_vel, sea_mask, line(obs_index), line(obs_value), line(obs_weight))
+    )(slabs, mean_state, *sides, east_vel, north_vel, sea_mask, line(obs_index), line(obs_value), line(obs_weight))
 
 
 def swap(value, axis, first):
@@ -471,7 +488,7 @@
     band, tile = ("x", "core"), ("z", "y")
     sides = [swap(lat_one, band, 0), swap(lat_two, band, 1), swap(lon_one, tile, 0), swap(lon_two, tile, 1)]
     advanced, keep, send = sums_of(
-        modes, mean_state, sides, east_vel, north_vel, sea_mask, obs_index, obs_value, obs_weight
+        slabs_of(modes), mean_state, sides, east_vel, north_vel, sea_mask, obs_index, obs_value, obs_weight
     )
     mine, other = sum_everywhere(keep, send)
     points = lat_rows * lon_cols * lax.axis_size(band) * lax.axis_size(tile)

time: 91.7 us -> 90.2 us (0.984)
  waiting for transfers between devices: 5.35 us -> 3.98 us
    ppermute x6, waiting for transfers between devices: 5.35 us -> 3.98 us  [swap(): return lax.ppermute(value, axis, pairs)]
    pallas_call x1 -> x2, Pallas kernels: 8.19 us -> 7.51 us  [the longest x1 6.33 us: sums_of(): pl.pallas_call(sums_kernel, in_specs=[VMEM] * 12, out_specs=[HBM] + [VMEM...]
  transfers between devices with their start and end apart: 6 -> 6, of which waited for: 4 -> 4; matrix products, arithmetic and copies ran while one was open for 0% -> 0% of each run, Pallas kernels for 0% -> 1%
where the time goes in v5:
time: 90.2 us; the launch traced here: 89.9 us
  blocking collectives  42.6 us (47%)
  Pallas kernels  29.8 us (33%)
  starting transfers between devices  11.5 us (13%)
  waiting for transfers between devices  3.98 us (4%)
  between operations  0.97 us (1%)
  local copies, waits for them, and re-layouts  0.94 us (1%)
    all_to_all x2, blocking collectives, gather(): lax.all_to_all(jnp.broadcast_to(value[None], (lax.axis_size(axes),) + val...  25.9 us
    pallas_call x1, Pallas kernels, finish(): pl.pallas_call(functools.partial(finish_kernel, scale), in_specs=[VMEM, V...  19.2 us
    all_to_all x1, blocking collectives, scatter_sum(): return lax.all_to_all(value.reshape(count, -1, LANES), axes, 0, 0).sum(0)  16.7 us
    ppermute x6, starting transfers between devices, swap(): return lax.ppermute(value, axis, pairs)  11.5 us
    pallas_call x1, Pallas kernels, sums_of(): pl.pallas_call(sums_kernel, in_specs=[VMEM] * 12, out_specs=[HBM] + [VMEM...  6.33 us
    ppermute x6, waiting for transfers between devices, swap(): return lax.ppermute(value, axis, pairs)  3.98 us
    pallas_call x1, Pallas kernels, edges_of(): pl.pallas_call(edges_kernel, in_specs=[HBM] * 2, out_specs=[VMEM] * 4, ou...  3.18 us
  transfers between devices with their start and end apart: 6, of which 4 were waited for; matrix products, arithmetic and copies ran while one was open for 0% of the time, Pallas kernels for 1%

profile of v5, /device:TPU:1, one launch (start us, length us, event | category | flops | bytes accessed | tf_op | source)
XLA Modules:
  0.0 89.9 jit_solution(17191260550423219903)
XLA Ops:
  0.6 0.0 copy-start
  0.6 0.9 copy-done.1
  1.5 3.2 %edges.1 = (f32[264,128]{1,0:T(8,128)S(1)}, f32[264,128]{1,0:T(8,128)S(1)}, f32[96,128]{1,0:T(8,128)S(1)}, f32[96,128]{1,0:T(8,128)S(1)}) custom-call(f32[256,32,128]{2,1,0:T(8,128)} %modes_ref.3, f32[32,128]{1,0:T(8,128)S(1)} %copy-done.1), custom_call_target="tpu_custom_call" | custom-call | tf_op jit(solution)/shard_map/edges/pallas_call | solution.py:107
  4.7 3.3 %collective-permute-start = (f32[264,128]{1,0:T(8,128)S(1)}, f32[264,128]{1,0:T(8,128)S(1)}, u32[]{:S(2)}, u32[]{:S(2)}) collective-permute-start(f32[264,128]{1,0:T(8,128)S(1)} %get-tuple-element.10), channel_id=1, source_target_pairs={{0,32},{64,96},{128,160},{192,224},{32,0},{96,64},{160,128},{224,1... | collective-permute-start | bytes 405512 | tf_op jit(solution)/shard_map/ppermute | solution.py:296
  8.0 1.9 %collective-permute-start.1 = (f32[264,128]{1,0:T(8,128)S(1)}, f32[264,128]{1,0:T(8,128)S(1)}, u32[]{:S(2)}, u32[]{:S(2)}) collective-permute-start(f32[264,128]{1,0:T(8,128)S(1)} %get-tuple-element.11), channel_id=1, source_target_pairs={{32,64},{96,128},{160,192},{64,32},{128,96},{192,160},{33,65},{97,... | collective-permute-start | bytes 405512 | tf_op jit(solution)/shard_map/ppermute | solution.py:296
  9.9 0.8 collective-permute-start.2
  10.7 0.0 copy-start.6
  10.7 0.0 copy-start.7
  10.7 0.8 collective-permute-start.3
  11.5 1.2 %slabs.1.slab_ref = f32[32,256,128]{2,1,0:T(8,128)S(1)} custom-call(f32[256,32,128]{2,1,0:T(8,128)S(1)} %copy-done), custom_call_target="tpu_custom_call" | custom-call | flops 4194304 | bytes 8388608 | tf_op jit(solution)/shard_map/slabs/pallas_call | solution.py:135
  12.7 0.2 collective-permute-done.2.lon_one
  13.0 0.0 collective-permute-done.3.lon_two
  13.0 0.0 collective-permute-done.lat_one
  13.0 1.4 %collective-permute-done.1.lat_two = f32[264,128]{1,0:T(8,128)S(1)} collective-permute-done((f32[264,128]{1,0:T(8,128)S(1)}, f32[264,128]{1,0:T(8,128)S(1)}, u32[]{:S(2)}, u32[]{:S(2)}) %collective-permute-start.1) | collective-permute-done | bytes 135200 | tf_op jit(solution)/shard_map/ppermute | solution.py:296
  14.3 0.0 copy-done.4
  14.4 6.3 %sums.1 = (f32[33,256,128]{2,1,0:T(8,128)}, f32[288,128]{1,0:T(8,128)S(1)}, f32[288,128]{1,0:T(8,128)S(1)}) custom-call(f32[32,256,128]{2,1,0:T(8,128)S(1)} %slabs.1.slab_ref, f32[32,128]{1,0:T(8,128)S(1)} %copy-done.1, f32[264,128]{1,0:T(8,128)S(1)} %collective-permute-done.lat_one, f32[264,128]{1,0:T(8,128)S(1)} %collective-permute-done.1.lat_two, ...), custom_call_target="tpu_custom_call" | custom-call | tf_op jit(solution)/shard_map/sums/pallas_call | solution.py:271
  20.7 0.1 collective-permute-start.4
  20.8 1.4 %collective-permute-done.4 = f32[288,128]{1,0:T(8,128)S(1)} collective-permute-done((f32[288,128]{1,0:T(8,128)S(1)}, f32[288,128]{1,0:T(8,128)S(1)}, u32[]{:S(2)}, u32[]{:S(2)}) %collective-permute-start.4) | collective-permute-done | bytes 147488 | tf_op jit(solution)/shard_map/ppermute | solution.py:296
  22.2 16.7 %all_to_all.15 = f32[16,18,128]{2,1,0:T(8,128)S(1)} all-to-all(f32[16,18,128]{2,1,0:T(8,128)S(1)} %reshape.26), channel_id=1, replica_groups=mesh['x'=4,'core'=2,'z'=8,'y'=4] {'x','y'}, dimensions={0} | all-to-all | bytes 294912 | tf_op jit(solution)/shard_map/all_to_all | solution.py:301
  39.0 15.7 %all_to_all.16 = f32[8,18,128]{2,1,0:T(8,128)S(1)} all-to-all(f32[8,18,128]{2,1,0:T(8,128)S(1)} %broadcast_in_dim.4), channel_id=1, replica_groups=mesh['x'=4,'core'=2,'z'=8,'y'=4] {'z'}, dimensions={0} | all-to-all | bytes 147456 | tf_op jit(solution)/shard_map/all_to_all | solution.py:305
  54.7 10.3 %all_to_all.17 = f32[16,18,128]{2,1,0:T(8,128)S(1)} all-to-all(f32[16,18,128]{2,1,0:T(8,128)S(1)} %broadcast_in_dim.5), channel_id=1, replica_groups=mesh['x'=4,'core'=2,'z'=8,'y'=4] {'x','y'}, dimensions={0} | all-to-all | bytes 294912 | tf_op jit(solution)/shard_map/all_to_all | solution.py:305
  65.0 4.6 %collective-permute-start.5 = (f32[288,128]{1,0:T(8,128)S(1)}, f32[288,128]{1,0:T(8,128)S(1)}, u32[]{:S(2)}, u32[]{:S(2)}) collective-permute-start(f32[288,128]{1,0:T(8,128)S(1)} %reshape.27.mine_ref), channel_id=1, source_target_pairs={{0,32},{32,0},{1,33},{33,1},{2,34},{34,2},{3,35},{35,3},{4,36},{36... | collective-permute-start | bytes 442376 | tf_op jit(solution)/shard_map/ppermute | solution.py:296
  69.5 1.0 %collective-permute-done.5.other_ref = f32[288,128]{1,0:T(8,128)S(1)} collective-permute-done((f32[288,128]{1,0:T(8,128)S(1)}, f32[288,128]{1,0:T(8,128)S(1)}, u32[]{:S(2)}, u32[]{:S(2)}) %collective-permute-start.5) | collective-permute-done | bytes 147488 | tf_op jit(solution)/shard_map/ppermute | solution.py:296
  70.6 19.2 %finish.1 = (f32[32,128]{1,0:T(8,128)}, f32[256,32,128]{2,1,0:T(8,128)}, f32[256,256]{1,0:T(8,128)}) custom-call(f32[288,128]{1,0:T(8,128)S(1)} %reshape.27.mine_ref, f32[288,128]{1,0:T(8,128)S(1)} %collective-permute-done.5.other_ref, f32[33,256,128]{2,1,0:T(8,128)} %get-tuple-element.16.adv_hbm), custom_call_target="tpu_custom_call" | custom-call | tf_op jit(solution)/shard_map/finish/pallas_call | solution.py:461
  (18 shorter events, 0.1 us)
Async XLA Ops:
  0.6 10.9 %copy-start = (f32[256,32,128]{2,1,0:T(8,128)S(1)}, f32[256,32,128]{2,1,0:T(8,128)}, u32[]{:S(2)}) copy-start(f32[256,32,128]{2,1,0:T(8,128)} %modes_ref.3) | copy-start | bytes 12582916
  0.6 0.9 copy-start.1
  4.7 8.3 %collective-permute-start = (f32[264,128]{1,0:T(8,128)S(1)}, f32[264,128]{1,0:T(8,128)S(1)}, u32[]{:S(2)}, u32[]{:S(2)}) collective-permute-start(f32[264,128]{1,0:T(8,128)S(1)} %get-tuple-element.10), channel_id=1, source_target_pairs={{0,32},{64,96},{128,160},{192,224},{32,0},{96,64},{160,128},{224,1... | collective-permute-start | bytes 405512 | tf_op jit(solution)/shard_map/ppermute | solution.py:296
  8.0 6.3 %collective-permute-start.1 = (f32[264,128]{1,0:T(8,128)S(1)}, f32[264,128]{1,0:T(8,128)S(1)}, u32[]{:S(2)}, u32[]{:S(2)}) collective-permute-start(f32[264,128]{1,0:T(8,128)S(1)} %get-tuple-element.11), channel_id=1, source_target_pairs={{32,64},{96,128},{160,192},{64,32},{128,96},{192,160},{33,65},{97,... | collective-permute-start | bytes 405512 | tf_op jit(solution)/shard_map/ppermute | solution.py:296
  9.9 3.0 %collective-permute-start.2 = (f32[96,128]{1,0:T(8,128)S(1)}, f32[96,128]{1,0:T(8,128)S(1)}, u32[]{:S(2)}, u32[]{:S(2)}) collective-permute-start(f32[96,128]{1,0:T(8,128)S(1)} %get-tuple-element.12), channel_id=1, source_target_pairs={{0,1},{2,3},{4,5},{6,7},{8,9},{10,11},{12,13},{14,15},{16,17},{18,... | collective-permute-start | bytes 147464 | tf_op jit(solution)/shard_map/ppermute | solution.py:296
  10.7 3.6 %copy-start.2 = (f32[32,128]{1,0:T(8,128)S(1)}, f32[32,128]{1,0:T(8,128)}, u32[]{:S(2)}) copy-start(f32[32,128]{1,0:T(8,128)} %uvel_ref.1) | copy-start | bytes 49156
  10.7 3.6 %copy-start.3 = (f32[32,128]{1,0:T(8,128)S(1)}, f32[32,128]{1,0:T(8,128)}, u32[]{:S(2)}) copy-start(f32[32,128]{1,0:T(8,128)} %vvel_ref.1) | copy-start | bytes 49156
  10.7 3.6 %copy-start.4 = (s32[32,128]{1,0:T(8,128)S(1)}, s32[32,128]{1,0:T(8,128)}, u32[]{:S(2)}) copy-start(s32[32,128]{1,0:T(8,128)} %mask_ref.1) | copy-start | bytes 49156
  10.7 3.7 %copy-start.5 = (s32[1,1,64]{2,1,0:T(1,128)S(1)}, s32[1,1,64]{2,1,0:T(1,128)}, u32[]{:S(2)}) copy-start(s32[1,1,64]{2,1,0:T(1,128)} %param.13) | copy-start | bytes 772
  10.7 3.7 %copy-start.6 = (f32[1,1,64]{2,1,0:T(1,128)S(1)}, f32[1,1,64]{2,1,0:T(1,128)}, u32[]{:S(2)}) copy-start(f32[1,1,64]{2,1,0:T(1,128)} %param.14) | copy-start | bytes 772
  10.7 3.7 %copy-start.7 = (f32[1,1,64]{2,1,0:T(1,128)S(1)}, f32[1,1,64]{2,1,0:T(1,128)}, u32[]{:S(2)}) copy-start(f32[1,1,64]{2,1,0:T(1,128)} %param.15) | copy-start | bytes 772
  10.7 2.2 %collective-permute-start.3 = (f32[96,128]{1,0:T(8,128)S(1)}, f32[96,128]{1,0:T(8,128)S(1)}, u32[]{:S(2)}, u32[]{:S(2)}) collective-permute-start(f32[96,128]{1,0:T(8,128)S(1)} %get-tuple-element.13), channel_id=1, source_target_pairs={{1,2},{3,4},{5,6},{7,8},{9,10},{11,12},{13,14},{15,16},{17,18},{19... | collective-permute-start | bytes 147464 | tf_op jit(solution)/shard_map/ppermute | solution.py:296
  20.7 1.5 %collective-permute-start.4 = (f32[288,128]{1,0:T(8,128)S(1)}, f32[288,128]{1,0:T(8,128)S(1)}, u32[]{:S(2)}, u32[]{:S(2)}) collective-permute-start(f32[288,128]{1,0:T(8,128)S(1)} %get-tuple-element.15), channel_id=1, source_target_pairs={{0,32},{32,0},{1,33},{33,1},{2,34},{34,2},{3,35},{35,3},{4,36},{36... | collective-permute-start | bytes 442376 | tf_op jit(solution)/shard_map/ppermute | solution.py:296
  65.0 5.6 %collective-permute-start.5 = (f32[288,128]{1,0:T(8,128)S(1)}, f32[288,128]{1,0:T(8,128)S(1)}, u32[]{:S(2)}, u32[]{:S(2)}) collective-permute-start(f32[288,128]{1,0:T(8,128)S(1)} %reshape.27.mine_ref), channel_id=1, source_target_pairs={{0,32},{32,0},{1,33},{33,1},{2,34},{34,2},{3,35},{35,3},{4,36},{36... | collective-permute-start | bytes 442376 | tf_op jit(solution)/shard_map/ppermute | solution.py:296
